TPU v7x, 256 devices: a whole 4x4x8 slice. The times are simulated.
256 devices in a mesh: batch: 8 (over x, core), seq: 32 (over y, z).
Axes of the slice: x: 4, y: 4, z: 8, core: 2. Of those that a mesh axis runs over, the one named last changes fastest.
Arguments:
- behaviors: bfloat16 [8, 8192, 1024], P('batch', 'seq'), may hold values from -100 to 100
- log_decay: float32 [8, 8, 8192], P('batch', None, 'seq'), may hold values from -1 to 0
- qkv_weight: bfloat16 [1024, 3072], replicated, may hold values from -0.1875 to 0.1875
- cotangent: bfloat16 [8, 8192, 1024], P('batch', 'seq'), may hold values from -6 to 6
Outputs:
- mixed: bfloat16 [8, 8192, 1024], P('batch', 'seq')
- d_behaviors: bfloat16 [8, 8192, 1024], P('batch', 'seq')
- weight_step: float32 [1024, 3072], P('seq')
All inputs are finite; a program needn't handle non-finite values.
Results may differ from a plain program's by a relative error of at most 0.0095.
Values sent between devices are 32-bit elements; how exact they have to be, the bound alone decides.
No kernel may reach another device: no remote copies, remote signals or barrier semaphores. Data moves between devices by JAX's collectives and lax.ppermute only.
A program may use at most 128 MiB of HBM per device.

v0:
```python
import functools

import jax
import jax.numpy as jnp
from jax import lax
from jax.experimental import pallas as pl
from jax.experimental.pallas import tpu as pltpu
from jax.sharding import PartitionSpec as P

epsilon = 1e-06
flt = jnp.float32
half = jnp.bfloat16
PAIR = 2
CORES = 2
EXTRA = 8
ORDER = ((0, 0), (1, 0), (3, 0), (2, 0), (0, 1), (1, 1), (2, 1), (3, 1))
FIRST = 3


def dot(a, b, ca, cb, precision=None):
    return lax.dot_general(
        a, b, (((ca,), (cb,)), ((), ())), preferred_element_type=flt, precision=precision
    )


def ordered(length):
    at = lax.broadcasted_iota(jnp.int32, (length, length), 0)
    source = lax.broadcasted_iota(jnp.int32, (length, length), 1)
    return at >= source


def running(rates):
    ones = ordered(rates.shape[1]).astype(flt)
    exact = lax.Precision.HIGHEST
    return dot(ones, rates, 1, 1, exact), dot(rates, ones, 1, 1, exact)


def decay_within(tall, flat, index):
    length = tall.shape[0]
    causal = ordered(length)
    spread = tall[:, index : index + 1] - flat[index : index + 1, :]
    return jnp.where(causal, jnp.exp(jnp.where(causal, spread, 0.0)), 0.0)


def place_in(index, step, count):
    return lax.rem(index + step + count, count)


def put_sum(sent_ref, lane, total):
    pieces = sent_ref.shape[0] // PAIR
    share = total.shape[0] // pieces
    for piece in range(pieces):
        sent_ref[lane * pieces + piece, :share, :] = total[piece * share : (piece + 1) * share]


def project_kernel(size, at_ref, rows_ref, wq_ref, wk_ref, wv_ref, rates_ref, q_ref, k_ref, v_ref,
                   tall_ref, flat_ref, sent_ref, top_ref, low_ref, own_ref, leaving_ref):
    step = pl.program_id(0)
    rows = rows_ref[...]
    width = top_ref.shape[1] // pl.num_programs(0)
    middle = top_ref.shape[0]
    columns = pl.ds(pl.multiple_of(step * width, width), width)
    top_ref[:, columns] = rows_ref[:middle, columns].astype(flt)
    low_ref[:, columns] = rows_ref[middle:, columns].astype(flt)
    for lane in range(PAIR):

        @pl.when(at_ref[0] == step * PAIR + lane)
        def _():
            for part, weight_ref in enumerate((wq_ref, wk_ref, wv_ref)):
                own_ref[:, part * size : (part + 1) * size] = weight_ref[:, lane * size : (lane + 1) * size]

    @pl.when(step == 0)
    def _():
        tall, flat = running(rates_ref[...])
        tall_ref[...] = tall
        flat_ref[...] = flat
        leaving_ref[...] = jnp.exp(tall[-1:] - tall)

    k = dot(rows, wk_ref[...], 1, 0).astype(half)
    v = dot(rows, wv_ref[...], 1, 0).astype(half)
    k_ref[...] = k
    v_ref[...] = v
    leaving = leaving_ref[...]
    lanes = lax.broadcasted_iota(jnp.int32, leaving.shape, 1)
    pieces = sent_ref.shape[0] // PAIR
    share = sent_ref.shape[1] - EXTRA
    for lane in range(PAIR):
        at = slice(lane * size, (lane + 1) * size)
        head = step * PAIR + lane
        column = jnp.sum(jnp.where(lanes == head, leaving, 0.0), axis=1, keepdims=True)
        keyed = (k[:, at].astype(flt) * column).astype(half)
        put_sum(sent_ref, lane, dot(keyed, v[:, at], 0, 0))
        last = flat_ref[pl.ds(head, 1), :][:, -1:]
        rate = jnp.broadcast_to(jnp.exp(last), (EXTRA, size))
        for piece in range(pieces):
            sent_ref[lane * pieces + piece, share:, :] = rate
    q_ref[...] = dot(rows, wq_ref[...], 1, 0).astype(half)


def scan_kernel(got_ref, mark_ref, out_ref, rates_ref):
    count, share, columns = out_ref.shape
    state = jnp.zeros((share, columns), flt)
    for block in range(count):
        out_ref[block] = state
        rates_ref[block] = got_ref[block, share:, :]
        state = got_ref[block, share : share + 1, :] * state + got_ref[block, :share, :]


def back_scan_kernel(got_ref, rates_ref, after_ref, out_ref, mark_ref):
    count, share, columns = out_ref.shape
    mark_ref[...] = after_ref[...] * 0.0
    state = jnp.zeros((share, columns), flt)
    for block in range(count - 1, -1, -1):
        out_ref[block] = state
        state = rates_ref[block, :1, :] * state + got_ref[block]


def column_of(table, index):
    lanes = lax.broadcasted_iota(jnp.int32, table.shape, 1)
    return jnp.sum(jnp.where(lanes == index, table, 0.0), axis=1, keepdims=True)


def decay_at(tall, flat_ref, index):
    length = tall.shape[0]
    causal = ordered(length)
    spread = column_of(tall, index) - flat_ref[pl.ds(index, 1), :]
    return jnp.where(causal, jnp.exp(jnp.where(causal, spread, 0.0)), 0.0)


def lanes_at(head, size):
    return pl.ds(pl.multiple_of(head * size, size), size)


def weights_kernel(heads, size, q_ref, k_ref, v_ref, tall_ref, flat_ref, weights_ref, intra_ref):
    tall = tall_ref[...]

    def one(head, _):
        at = lanes_at(head, size)
        scores = dot(q_ref[:, at], k_ref[:, at], 1, 1)
        weights = (scores * decay_at(tall, flat_ref, head)).astype(half)
        weights_ref[head] = weights
        intra_ref[:, at] = dot(weights, v_ref[:, at], 1, 0)

    lax.fori_loop(0, heads, one, None)


def mix_kernel(size, q_ref, intra_ref, up_ref, tall_ref, state_ref, after_ref, mixed_ref, dout_ref, sent_ref):
    heads = state_ref.shape[0]
    pieces = sent_ref.shape[0] // heads
    share = size // pieces
    entering = jnp.exp(tall_ref[...])

    def one(head, _):
        at = lanes_at(head, size)
        q = q_ref[:, at]
        column = column_of(entering, head)
        output = intra_ref[:, at] + dot(q, state_ref[head].astype(half), 1, 0) * column
        scale = lax.rsqrt(jnp.mean(output * output, axis=-1, keepdims=True) + epsilon)
        normed = output * scale
        mixed_ref[:, at] = normed.astype(half)
        incoming = up_ref[:, at].astype(flt)
        along = jnp.mean(normed * incoming, axis=-1, keepdims=True)
        d_output = (scale * (incoming - normed * along)).astype(half)
        dout_ref[:, at] = d_output
        lifted = (q.astype(flt) * column).astype(half)
        total = dot(lifted, d_output, 0, 0)
        for piece in range(pieces):
            sent_ref[head * pieces + piece] = total[piece * share : (piece + 1) * share]

    lax.fori_loop(0, heads, one, None, unroll=2)


def head_at(at_ref, step, turn, chips):
    chip, core = at_ref[0] // CORES, lax.rem(at_ref[0], CORES)
    return place_in(chip, step, chips) * CORES + lax.rem(core + turn, CORES)


def pack_kernel(size, at_ref, dout_ref, state_ref, rates_ref, own_ref, other_ref):
    length = dout_ref.shape[0]
    chips = own_ref.shape[0]
    for turn, out_ref in enumerate((own_ref, other_ref)):
        for step in range(chips):
            head = head_at(at_ref, step, turn, chips)
            columns = pl.ds(pl.multiple_of(head * size, size), size)
            out_ref[step, :length, :] = dout_ref[:, columns].astype(flt)
            out_ref[step, length : length + size, :] = state_ref[head]
            row = rates_ref[pl.ds(head, 1), :]
            out_ref[step, length + size :, :] = jnp.zeros((EXTRA, size), flt)
            for part in range(length // size):
                to = length + size + part
                out_ref[step, to : to + 1, :] = row[:, part * size : (part + 1) * size]


def pair_kernel(own_ref, came_ref, *out_refs):
    for step, out_ref in enumerate(out_refs):
        out_ref[0] = own_ref[step]
        out_ref[1] = came_ref[step]


def recall_kernel(weight_ref, after_ref, *refs):
    wide_refs, (rows_ref, qkv_ref, mark_ref, held_ref, sem) = refs[:-5], refs[-5:]
    count, length, _ = rows_ref.shape
    middle = length // 2
    copies = [
        pltpu.make_async_copy(wide_ref, held_ref.at[part // 2, pl.ds(part % 2 * middle, middle)], sem.at[part])
        for part, wide_ref in enumerate(wide_refs)
    ]
    for copy in copies:
        copy.start()
    mark_ref[...] = jnp.zeros(mark_ref.shape, flt)

    def one(place, _):
        for part in range(2):
            target = held_ref.at[place, pl.ds(part * middle, middle)]
            pltpu.make_async_copy(wide_refs[0], target, sem.at[2 * place + part]).wait()
        rows = held_ref[place].astype(half)
        rows_ref[place] = rows
        qkv_ref[place] = dot(rows, weight_ref[...], 1, 0).astype(half)

    lax.fori_loop(0, count, one, None)


def inner_grads(q, k, v, d_output, weights, state, within, entering):
    d_score = (dot(d_output, v, 1, 1) * within).astype(half)
    d_query = dot(d_score, k, 1, 0) + entering * dot(d_output, state, 1, 1)
    return d_query.astype(half), dot(d_score, q, 0, 0), dot(weights, d_output, 0, 0)


def owner_kernel(size, first_ref, rest_ref, *refs):
    got_refs, (tall_ref, turned_ref, dk_ref, dv_ref, flat_held, got_held) = refs[:-6], refs[-6:]
    length = first_ref.shape[1]
    base = length + size
    gots = [got_refs[step].at[turn] for step, turn in ORDER]
    rates = jnp.concatenate(
        [
            jnp.concatenate([got[base + part : base + part + 1, :] for part in range(length // size)], axis=1)
            for got in gots
        ],
        axis=0,
    )
    tall, flat = running(rates)
    tall_ref[...] = tall
    flat_held[...] = flat
    for place, got in enumerate(gots):
        got_held[place] = got[:base, :]
    entering = jnp.exp(tall)

    def one(place, qkv):
        q, k, v = (qkv[:, part * size : (part + 1) * size] for part in range(3))
        within = decay_at(tall, flat_held, place)
        weights = (dot(q, k, 1, 1) * within).astype(half)
        d_output = got_held[place, :length, :].astype(half)
        state = got_held[place, length:, :].astype(half)
        d_query, dk_ref[place], dv_ref[place] = inner_grads(
            q, k, v, d_output, weights, state, within, column_of(entering, place)
        )
        turned_ref[:, lanes_at(place, length)] = d_query.T

    lax.fori_loop(0, FIRST, lambda place, _: one(place, first_ref[place]), None)
    lax.fori_loop(FIRST, len(ORDER), lambda place, _: one(place, rest_ref[place - FIRST]), None)


def late_kernel(size, first_ref, rest_ref, dk_ref, dv_ref, tall_ref, dq_ref, *refs):
    refs[-2][:size, :] = dq_ref[...]
    back_refs, (out_ref, held_ref) = refs[:-2], refs[-2:]
    length = first_ref.shape[1]
    tall = tall_ref[...]
    leaving = jnp.exp(tall[-1:] - tall)
    for place, (step, turn) in enumerate(ORDER):
        held_ref[place] = back_refs[step][turn].astype(half)

    def one(place, k, v):
        column = column_of(leaving, place)
        back = held_ref[place]
        d_key = (dk_ref[place] + column * dot(v, back, 1, 1)).astype(half)
        d_value = (dv_ref[place] + column * dot(k, back, 1, 0)).astype(half)
        out_ref[size : 2 * size, lanes_at(place, length)] = d_key.T
        out_ref[2 * size :, lanes_at(place, length)] = d_value.T

    def near(place, _):
        one(place, first_ref[place, :, size : 2 * size], first_ref[place, :, 2 * size :])

    def far(place, _):
        at = place - FIRST
        one(place, rest_ref[at, :, size : 2 * size], rest_ref[at, :, 2 * size :])

    lax.fori_loop(0, FIRST, near, None)
    lax.fori_loop(FIRST, len(ORDER), far, None)


def choose_kernel(at_ref, back_ref, after_ref, own_ref, other_ref, keep_ref):
    chips = own_ref.shape[0]
    for step in range(chips):
        own_ref[step] = back_ref[head_at(at_ref, step, 0, chips)]
        other_ref[step] = back_ref[head_at(at_ref, step, 1, chips)]
    keep_ref[...] = back_ref[...].astype(half)


def term_kernel(step, at_ref, turned_ref, first_ref, rest_ref, out_ref):
    _, length, width = first_ref.shape
    users = len(ORDER)
    share = out_ref.shape[1]
    target = place_in(at_ref[1] // users, step, width // share)
    columns = pl.ds(pl.multiple_of(target * share, share), share)
    middle = FIRST * length
    first = first_ref[:, :, columns].reshape(middle, share)
    rest = rest_ref[:, :, columns].reshape(users * length - middle, share)
    out_ref[...] = dot(turned_ref[:, :middle], first, 1, 0) + dot(turned_ref[:, middle:], rest, 1, 0)


def fold_kernel(at_ref, *refs):
    got_refs, out_refs, slots_ref = refs[:4], refs[5:-1], refs[-1]
    blocks = len(out_refs)
    total = got_refs[0][...]
    for got_ref in got_refs[1:]:
        total += got_ref[...]
    turned = total.T
    line = lax.rem(at_ref[1], blocks)
    share = turned.shape[0] // blocks
    for block in range(blocks):
        slots_ref[block] = turned[block * share : (block + 1) * share]
    for step, out_ref in enumerate(out_refs):
        out_ref[...] = slots_ref[place_in(line, step, blocks)]


def gather_kernel(*refs):
    total = refs[0][...]
    for got_ref in refs[1:-1]:
        total += got_ref[...]
    refs[-1][...] = total


def both_kernel(mine_ref, other_ref, out_ref):
    out_ref[0] = mine_ref[...]
    out_ref[1] = other_ref[...]


def square_kernel(*refs):
    got_refs, out_ref = refs[:-1], refs[-1]
    size = out_ref.shape[2]
    for part in range(3):
        total = jnp.zeros((1, size), flt)
        for got_ref in got_refs:
            for core in range(CORES):
                piece = got_ref[core, :, part * size : (part + 1) * size]
                total += jnp.sum(piece * piece, axis=0, keepdims=True)
        out_ref[:, part : part + 1, :] = jnp.broadcast_to(total[None], (out_ref.shape[0], 1, size))
    out_ref[:, 3:, :] = jnp.zeros((out_ref.shape[0], EXTRA - 3, size), flt)


def step_kernel(at_ref, squares_ref, *refs):
    got_refs, out_ref, slots_ref = refs[:-2], refs[-2], refs[-1]
    heads, share, width = slots_ref.shape
    size = width // 3
    chips = heads // CORES
    chip, core = at_ref[0] // CORES, lax.rem(at_ref[0], CORES)
    for step, got_ref in enumerate(got_refs):
        for turn in range(CORES):
            head = place_in(chip, -step, chips) * CORES + lax.rem(core + turn, CORES)
            slots_ref[head] = got_ref[turn]
    total = jnp.sum(squares_ref[...], axis=0)
    entries = float(heads * size) ** 2
    for part in range(3):
        mean = jnp.sum(total[part : part + 1], axis=1, keepdims=True) / entries
        factor = lax.rsqrt(mean + epsilon)
        for head in range(heads):
            at = (part * heads + head) * size
            out_ref[:, at : at + size] = slots_ref[head, :, part * size : (part + 1) * size] * factor


def rows_kernel(size, dq_ref, dki_ref, dvi_ref, k_ref, v_ref, back_ref, tall_ref,
                wq_ref, wk_ref, wv_ref, out_ref, dk_ref, dv_ref):
    @pl.when(pl.program_id(0) == 0)
    def _():
        tall = tall_ref[...]
        leaving = jnp.exp(tall[-1:] - tall)
        for head in range(back_ref.shape[0]):
            at = slice(head * size, (head + 1) * size)
            column = leaving[:, head : head + 1]
            back = back_ref[head]
            dk_ref[:, at] = (dki_ref[:, at] + column * dot(v_ref[:, at], back, 1, 1)).astype(half)
            dv_ref[:, at] = (dvi_ref[:, at] + column * dot(k_ref[:, at], back, 1, 0)).astype(half)

    total = dot(dq_ref[...], wq_ref[...], 1, 1)
    total += dot(dk_ref[...], wk_ref[...], 1, 1)
    total += dot(dv_ref[...], wv_ref[...], 1, 1)
    out_ref[...] = total.astype(half)


def inner_kernel(size, q_ref, k_ref, v_ref, dout_ref, weights_ref, state_ref, tall_ref, flat_ref,
                 dq_ref, dk_ref, dv_ref):
    tall = tall_ref[...]
    entering = jnp.exp(tall)

    def one(head, _):
        at = lanes_at(head, size)
        dq_ref[:, at], dk_ref[:, at], dv_ref[:, at] = inner_grads(
            q_ref[:, at], k_ref[:, at], v_ref[:, at], dout_ref[:, at], weights_ref[head],
            state_ref[head].astype(half), decay_at(tall, flat_ref, head), column_of(entering, head)
        )

    lax.fori_loop(0, weights_ref.shape[0], one, None)


def shape(dims, kind=flt):
    return jax.ShapeDtypeStruct(dims, kind)


def kernel(body, out_shape, flops, moved, name, placed=True, limit=16, after=None, **more):
    cost = pl.CostEstimate(flops=int(flops), bytes_accessed=int(moved), transcendentals=0)
    settings = dict(
        out_shape=out_shape,
        compiler_params=pltpu.CompilerParams(vmem_limit_bytes=limit << 20),
        cost_estimate=cost,
        name=name,
    )
    settings.update(more)

    def space(place):
        if after is not None and place >= after:
            return pl.ANY
        return pltpu.SMEM if placed and place == 0 else pltpu.VMEM

    return lambda *arrays: pl.pallas_call(
        body,
        in_specs=[pl.BlockSpec(memory_space=space(place)) for place in range(len(arrays))],
        **settings,
    )(*arrays)


def on_device(behaviors, log_decay, qkv_weight, cotangent):
    rows = behaviors[0]
    rates = log_decay[0]
    upstream = cotangent[0]
    length, width = rows.shape
    heads = rates.shape[0]
    size = width // heads
    users = lax.axis_size("batch")
    count = lax.axis_size("seq")
    segments = count // heads
    chips = users // CORES
    pairs = heads // PAIR
    wide = PAIR * size
    at = jnp.stack([lax.axis_index("batch"), lax.axis_index("seq")]).astype(jnp.int32)

    def along_line(array, step):
        pairs_of = [(s, s // heads * heads + (s + step) % heads) for s in range(count)]
        return lax.ppermute(array, "seq", pairs_of)

    def along_segments(array, step):
        return lax.ppermute(array, "seq", [(s, (s + step * heads) % count) for s in range(count)])

    def along_users(array, step, turn):
        pairs_of = [
            (u, (u // CORES + step) % chips * CORES + (u + turn) % CORES) for u in range(users)
        ]
        return lax.ppermute(array, "batch", pairs_of)

    def line_exchange(arrays):
        return [arrays[0]] + [along_line(arrays[step], step) for step in range(1, heads)]

    whole = lambda dims: pl.BlockSpec(dims, lambda i: (0,) * len(dims))
    column = pl.BlockSpec((length, wide), lambda i: (0, i))
    weight_at = lambda part: pl.BlockSpec((width, wide), lambda i: (0, part * pairs + i))
    tokens = lambda kind: shape((length, width), kind)
    state = shape((size, size))
    smem = pl.BlockSpec(memory_space=pltpu.SMEM)
    share = heads * size // count
    slices = shape((count, share, size))
    square = length * length * size

    def exchange(own, other, moved):
        dims = own.shape[1:]
        came = along_users(other, 0, 1)
        both = kernel(
            pair_kernel, [shape((CORES,) + dims)] * chips, 1 << 16, moved, "pair", False
        )(own, came)
        return [both[0]] + [along_users(both[step], step, 0) for step in range(1, chips)]

    q, k, v, tall, flat, sums, top, low, weight_columns = pl.pallas_call(
        functools.partial(project_kernel, size),
        grid=(pairs,),
        in_specs=[smem, whole((length, width)), weight_at(0), weight_at(1), weight_at(2), whole((heads, length))],
        out_specs=[column] * 3 + [whole((length, heads)), whole((heads, length))]
        + [pl.BlockSpec((count // pairs, share + EXTRA, size), lambda i: (i, 0, 0))]
        + [whole((length // 2, width))] * 2 + [whole((width, 3 * size))],
        out_shape=[tokens(half)] * 3 + [shape((length, heads)), shape((heads, length))]
        + [shape((count, share + EXTRA, size))] + [shape((length // 2, width))] * 2
        + [shape((width, 3 * size), half)],
        scratch_shapes=[pltpu.VMEM((length, heads), flt)],
        compiler_params=pltpu.CompilerParams(vmem_limit_bytes=59 << 20),
        cost_estimate=pl.CostEstimate(
            flops=6 * length * width * width, bytes_accessed=8 * width * width, transcendentals=0
        ),
        name="project",
    )(at, rows, qkv_weight, qkv_weight, qkv_weight, rates)
    ahead, astern = (lambda array: along_users(array, 1, 0)), (lambda array: along_users(array, chips - 1, 0))
    top_before, low_behind = ahead(top), astern(low)
    low_before, top_behind = ahead(low), astern(top)
    top_beyond, low_beyond = ahead(top_before), astern(low_behind)
    near_wide = [top, low, top_before, low_before, top_beyond, low_beyond, top_behind, low_behind]
    far_wide = [along_users(array, 0, 1) for array in near_wide]

    def mark_of(*arrays):
        return sum(array[-EXTRA:, :size] for array in arrays)

    got = lax.all_to_all(sums, "seq", 0, 0)
    entered, block_rates = kernel(
        scan_kernel, [slices, shape((count, EXTRA, size))], 1 << 18, 1 << 20, "scan", False
    )(got, mark_of(top_before, low_behind))
    state_in = lax.all_to_all(entered, "seq", 0, 0).reshape(heads, size, size)

    weights, intra = kernel(
        functools.partial(weights_kernel, heads, size),
        [shape((heads, length, length), half), tokens(flt)],
        heads * 4 * square, 5 << 20, "weights", False,
    )(q, k, v, tall, flat)

    mixed, d_output, sums = kernel(
        functools.partial(mix_kernel, size),
        [tokens(half), tokens(half), slices],
        heads * 2 * square, 5 << 20, "mix", False,
    )(q, intra, upstream, tall, state_in, mark_of(low_before, top_behind))
    got = lax.all_to_all(sums, "seq", 0, 0)
    packed = kernel(
        functools.partial(pack_kernel, size),
        [shape((chips, length + size + EXTRA, size))] * CORES, 1 << 18, 3 << 20, "pack",
    )(at, d_output, state_in, rates)
    every = exchange(*packed, 3 << 20)

    def recall(wide, after, name):
        count = len(wide) // 2
        return kernel(
            recall_kernel,
            [shape((count, length, width), half), shape((count, length, 3 * size), half), shape((EXTRA, size))],
            6 * length * width * size * count, 8 << 20, name, False, after=2, limit=50,
            scratch_shapes=[pltpu.VMEM((count, length, width), flt), pltpu.SemaphoreType.DMA((2 * count,))],
        )(weight_columns, after, *wide)

    pieces = {(step, 0): near_wide[2 * step : 2 * step + 2] for step in range(chips)}
    pieces.update({(step, 1): far_wide[2 * step : 2 * step + 2] for step in range(chips)})
    wides = [piece for place in ORDER for piece in pieces[place]]
    first_rows, first_qkv, mark = recall(wides[: 2 * FIRST], mark_of(top_before), "recall")

    entered, mark = kernel(
        back_scan_kernel, [slices, shape((EXTRA, size))], 1 << 18, 1 << 20, "back_scan", False
    )(got, block_rates, mark + mark_of(top_beyond, low_beyond))
    back = lax.all_to_all(entered, "seq", 0, 0).reshape(heads, size, size)
    d_query, key_part, value_part = kernel(
        functools.partial(inner_kernel, size),
        [tokens(half), tokens(flt), tokens(flt)], heads * 10 * square, 6 << 20, "inner", False,
    )(q, k, v, d_output, weights, state_in, tall, flat)
    rest_rows, rest_qkv, mark = recall(wides[2 * FIRST :], mark, "recall_rest")
    *chosen, back_bf = kernel(
        choose_kernel, [shape((chips, size, size))] * CORES + [shape((heads, size, size), half)],
        1 << 18, 1 << 20, "choose",
    )(at, back, mark)
    owned = exchange(*chosen, 1 << 20)

    owner_tall, turned_query, key_inner, value_inner = kernel(
        functools.partial(owner_kernel, size),
        [shape((length, users)), shape((size, users * length), half)] + [shape((users, length, size))] * 2,
        users * 12 * square, 6 << 20, "owner", False,
        scratch_shapes=[pltpu.VMEM((users, length), flt), pltpu.VMEM((users, length + size, size), flt)],
    )(first_qkv, rest_qkv, *every)
    turned = kernel(
        functools.partial(late_kernel, size),
        shape((3 * size, users * length), half), users * 2 * square, 4 << 20, "late", False,
        scratch_shapes=[pltpu.VMEM((users, size, size), half)],
    )(first_qkv, rest_qkv, key_inner, value_inner, owner_tall, turned_query, *owned)

    weight_rows = lambda part: pl.BlockSpec((wide, width), lambda i: (i, part))
    d_rows = pl.pallas_call(
        functools.partial(rows_kernel, size),
        grid=(pairs,),
        in_specs=[whole((length, width))] * 5
        + [whole((heads, size, size)), whole((length, heads))]
        + [weight_rows(part) for part in range(3)],
        out_specs=column,
        out_shape=tokens(half),
        scratch_shapes=[pltpu.VMEM((length, width), half)] * 2,
        compiler_params=pltpu.CompilerParams(vmem_limit_bytes=24 << 20),
        cost_estimate=pl.CostEstimate(
            flops=6 * length * width * width, bytes_accessed=8 * width * width, transcendentals=0
        ),
        name="rows",
    )(d_query, key_part, value_part, k, v, back_bf, tall, qkv_weight, qkv_weight, qkv_weight)
    def term(step):
        return kernel(
            functools.partial(term_kernel, step),
            shape((3 * size, width // segments)),
            6 * users * length * size * width // segments, 3 << 20, "term",
        )(at, turned, first_rows, rest_rows)

    got = [along_segments(term(step), step) for step in (2, 1, 3)] + [term(0)]
    pieces = kernel(
        fold_kernel, [shape((width // count, 3 * size))] * heads, 1 << 20, 2 << 20, "fold",
        scratch_shapes=[pltpu.VMEM((heads, width // count, 3 * size), flt)], after=5,
    )(at, *got, d_rows)
    got = line_exchange(pieces)
    mine = kernel(gather_kernel, shape((width // count, 3 * size)), 1 << 18, 1 << 18, "gather", False)(*got)

    other = along_users(mine, 0, 1)
    both = kernel(both_kernel, shape((CORES, width // count, 3 * size)), 1 << 16, 1 << 17, "both", False)(mine, other)
    summed = [both] + [along_users(both, step, 0) for step in range(1, chips)]
    squares = kernel(square_kernel, shape((count, EXTRA, size)), 1 << 18, 1 << 18, "square", False)(*summed)
    squares = lax.all_to_all(squares, "seq", 0, 0)
    weight_step = kernel(
        step_kernel, shape((width // count, 3 * width)), 1 << 18, 1 << 20, "step",
        scratch_shapes=[pltpu.VMEM((heads, width // count, 3 * size), flt)],
    )(at, squares, *summed)

    return (mixed[None], d_rows[None], weight_step)


def solution(mesh):
    placed = (P("batch", "seq", None), P("batch", None, "seq"), P(), P("batch", "seq", None))
    return jax.shard_map(
        on_device,
        mesh=mesh,
        in_specs=placed,
        out_specs=(P("batch", "seq", None), P("batch", "seq", None), P("seq", None)),
        check_vma=False,
    )
```

profile of v0, /device:TPU:32, one launch (start us, length us, event | category | flops | bytes accessed | tf_op | source)
XLA Modules:
  0.0 221.7 jit_solution(6936837083959714127)
XLA Ops:
  1.2 8.4 %project.1 = (bf16[256,1024]{1,0:T(8,128)(2,1)}, bf16[256,1024]{1,0:T(8,128)(2,1)}, bf16[256,1024]{1,0:T(8,128)(2,1)}, f32[256,8]{1,0:T(8,128)}, f32[8,256]{1,0:...) custom-call(s32[2]{0:T(128)} %pad_add_fusion.at_ref, ...), custom_call_target="tpu_custom_call" | custom-call | flops 1610612736 | bytes 8388608 | tf_op jit(solution)/shard_map/project/pallas_call | solution.py:480
  9.7 11.5 %all-to-all-start = ((f32[32,40,128]{2,1,0:T(8,128)}), f32[32,40,128]{2,1,0:T(8,128)S(1)}, u32[]{:S(2)}, u32[]{:S(2)}) async-start(f32[32,40,128]{2,1,0:T(8,128)} %get-tuple-element.61), calls=%async_computation | async-start | bytes 1310720 | tf_op jit(solution)/shard_map/all_to_all | solution.py:507
  21.2 1.5 collective-permute-start
  22.7 1.8 collective-permute-start.1
  24.5 11.3 %collective-permute-done.refs_2_ = f32[128,1024]{1,0:T(8,128)S(1)} collective-permute-done((f32[128,1024]{1,0:T(8,128)}, f32[128,1024]{1,0:T(8,128)S(1)}, u32[]{:S(2)}, u32[]{:S(2)}) %collective-permute-start) | collective-permute-done | bytes 524320 | tf_op jit(solution)/shard_map/ppermute | solution.py:457
  36.6 4.9 %all-to-all-done.got_ref = f32[32,40,128]{2,1,0:T(8,128)S(1)} async-done(((f32[32,40,128]{2,1,0:T(8,128)}), f32[32,40,128]{2,1,0:T(8,128)S(1)}, u32[]{:S(2)}, u32[]{:S(2)}) %all-to-all-start) | async-done | bytes 655392 | tf_op jit(solution)/shard_map/all_to_all | solution.py:507
  42.3 5.7 %all-to-all-start.1 = ((f32[32,32,128]{2,1,0:T(8,128)}), f32[32,32,128]{2,1,0:T(8,128)S(1)}, u32[]{:S(2)}, u32[]{:S(2)}) async-start(f32[32,32,128]{2,1,0:T(8,128)} %copy-done.31), calls=%async_computation.1 | async-start | bytes 1048576 | tf_op jit(solution)/shard_map/all_to_all | solution.py:511
  48.0 2.2 %collective-permute-start.3 = (f32[128,1024]{1,0:T(8,128)}, f32[128,1024]{1,0:T(8,128)}, u32[]{:S(2)}, u32[]{:S(2)}) collective-permute-start(f32[128,1024]{1,0:T(8,128)} %get-tuple-element.62.refs_0_), channel_id=1, source_target_pairs={{0,192},{32,224},{64,0},{96,32},{128,64},{160,96},{192,128},{224,1... | collective-permute-start | bytes 1572872 | tf_op jit(solution)/shard_map/ppermute | solution.py:457
  50.4 2.7 %weights.1 = (bf16[8,256,256]{2,1,0:T(8,128)(2,1)S(1)}, f32[256,1024]{1,0:T(8,128)S(1)}) custom-call(bf16[256,1024]{1,0:T(8,128)(2,1)S(1)} %copy-done.4, bf16[256,1024]{1,0:T(8,128)(2,1)S(1)} %copy-done.2, bf16[256,1024]{1,0:T(8,128)(2,1)S(1)} %copy-done.3, f32[256,8]{1,0:T(8,128)S(1)} %copy-done.9, f32[8,256]{1,0:T(8,128)S(1)} %copy-done.37), custom_call_target="tpu_custom_call" | custom-call | flops 268435456 | bytes 5242880 | tf_op jit(solution)/shard_map/weights/pallas_call | solution.py:424
  55.1 5.6 %collective-permute-done.3.refs_4_ = f32[128,1024]{1,0:T(8,128)} collective-permute-done((f32[128,1024]{1,0:T(8,128)}, f32[128,1024]{1,0:T(8,128)}, u32[]{:S(2)}, u32[]{:S(2)}) %collective-permute-start.3) | collective-permute-done | bytes 524320 | tf_op jit(solution)/shard_map/ppermute | solution.py:457
  60.6 3.1 %collective-permute-done.2.refs_3_ = f32[128,1024]{1,0:T(8,128)S(1)} collective-permute-done((f32[128,1024]{1,0:T(8,128)S(1)}, f32[128,1024]{1,0:T(8,128)S(1)}, u32[]{:S(2)}, u32[]{:S(2)}) %collective-permute-start.2) | collective-permute-done | bytes 524320 | tf_op jit(solution)/shard_map/ppermute | solution.py:457
  65.2 1.2 copy-done.11
  67.5 2.8 %mix.1 = (bf16[256,1024]{1,0:T(8,128)(2,1)}, bf16[256,1024]{1,0:T(8,128)(2,1)S(1)}, f32[32,32,128]{2,1,0:T(8,128)S(1)}) custom-call(bf16[256,1024]{1,0:T(8,128)(2,1)S(1)} %copy-done.4, f32[256,1024]{1,0:T(8,128)S(1)} %copy-done.11, bf16[256,1024]{1,0:T(8,128)(2,1)S(1)} %bitcast.16, f32[256,8]{1,0:T(8,128)S(1)} %copy-done.9, f32[8,128,128]{2,1,0:T(8,128)S(1)} %bitcast.11, ...), custom_call_target="tpu_custom_call" | custom-call | flops 134217728 | bytes 5242880 | tf_op jit(solution)/shard_map/mix/pallas_call | solution.py:424
  71.1 9.8 %all-to-all-start.2 = ((f32[32,32,128]{2,1,0:T(8,128)}), f32[32,32,128]{2,1,0:T(8,128)S(1)}, u32[]{:S(2)}, u32[]{:S(2)}) async-start(f32[32,32,128]{2,1,0:T(8,128)} %copy-done.30), calls=%async_computation.2 | async-start | bytes 1048576 | tf_op jit(solution)/shard_map/all_to_all | solution.py:524
  81.0 3.2 %collective-permute-start.5 = (f32[128,1024]{1,0:T(8,128)}, f32[128,1024]{1,0:T(8,128)S(1)}, u32[]{:S(2)}, u32[]{:S(2)}) collective-permute-start(f32[128,1024]{1,0:T(8,128)} %copy-done.16), channel_id=1, source_target_pairs={{0,192},{32,224},{64,0},{96,32},{128,64},{160,96},{192,128},{224,1... | collective-permute-start | bytes 1572872 | tf_op jit(solution)/shard_map/ppermute | solution.py:457
  84.2 1.7 pack.1
  92.5 3.8 %recall.1 = (bf16[3,256,1024]{2,1,0:T(8,128)(2,1)}, bf16[3,256,384]{2,1,0:T(8,128)(2,1)S(1)}, f32[8,128]{1,0:T(8,128)S(1)}) custom-call(bf16[1024,384]{1,0:T(8,128)(2,1)} %get-tuple-element.73.weight_ref, f32[8,128]{1,0:T(8,128)S(1)} %get-tuple-element.107.after_ref, f32[128,1024]{1,0:T(8,128)S(1)} %copy-done.28, f32[128,1024]{1,0:T(8,128)S(1)} %copy-done.27, ...), custom_call_target="tpu_custom_call" | custom-call | flops 603979776 | bytes 8388608 | tf_op jit(solution)/shard_map/recall/pallas_call | solution.py:424
  98.5 9.8 %all-to-all-start.3 = ((f32[32,32,128]{2,1,0:T(8,128)}), f32[32,32,128]{2,1,0:T(8,128)S(1)}, u32[]{:S(2)}, u32[]{:S(2)}) async-start(f32[32,32,128]{2,1,0:T(8,128)} %copy-done.29), calls=%async_computation.3 | async-start | bytes 1048576 | tf_op jit(solution)/shard_map/all_to_all | solution.py:548
  110.7 2.3 %pair.2 = (f32[2,392,128]{2,1,0:T(8,128)S(1)}, f32[2,392,128]{2,1,0:T(8,128)}, f32[2,392,128]{2,1,0:T(8,128)}, f32[2,392,128]{2,1,0:T(8,128)}) custom-call(f32[4,392,128]{2,1,0:T(8,128)S(1)} %copy-done.15, f32[4,392,128]{2,1,0:T(8,128)} %collective-permute-done.14.came_ref), custom_call_target="tpu_custom_call" | custom-call | flops 65536 | bytes 3145728 | tf_op jit(solution)/shard_map/pair/pallas_call | solution.py:424
  113.7 1.5 collective-permute-start.16
  115.2 1.9 collective-permute-start.17
  120.0 6.0 %recall_rest.1 = (bf16[5,256,1024]{2,1,0:T(8,128)(2,1)}, bf16[5,256,384]{2,1,0:T(8,128)(2,1)}, f32[8,128]{1,0:T(8,128)S(1)}) custom-call(bf16[1024,384]{1,0:T(8,128)(2,1)} %get-tuple-element.73.weight_ref, f32[8,128]{1,0:T(8,128)S(1)} %get-tuple-element.76.after_ref, f32[128,1024]{1,0:T(8,128)S(1)} %copy-done.23, f32[128,1024]{1,0:T(8,128)S(1)} %copy-done.25, ...), custom_call_target="tpu_custom_call" | custom-call | flops 1006632960 | bytes 8388608 | tf_op jit(solution)/shard_map/recall_rest/pallas_call | solution.py:424
  126.9 1.5 collective-permute-done.18.came_ref
  129.2 2.0 collective-permute-start.20
  131.2 4.7 %collective-permute-done.15.refs_1_ = f32[2,392,128]{2,1,0:T(8,128)} collective-permute-done((f32[2,392,128]{2,1,0:T(8,128)}, f32[2,392,128]{2,1,0:T(8,128)}, u32[]{:S(2)}, u32[]{:S(2)}) %collective-permute-start.15) | collective-permute-done | bytes 401440 | tf_op jit(solution)/shard_map/ppermute | solution.py:457
  136.9 1.2 copy-done.5
  139.1 5.9 %owner.1 = (f32[256,8]{1,0:T(8,128)S(1)}, bf16[128,2048]{1,0:T(8,128)(2,1)S(1)}, f32[8,256,128]{2,1,0:T(8,128)S(1)}, f32[8,256,128]{2,1,0:T(8,128)S(1)}) custom-call(bf16[3,256,384]{2,1,0:T(8,128)(2,1)S(1)} %get-tuple-element.79.first_ref, bf16[5,256,384]{2,1,0:T(8,128)(2,1)S(1)} %copy-done.5, f32[2,392,128]{2,1,0:T(8,128)S(1)} %copy-done.34, ...), custom_call_target="tpu_custom_call" | custom-call | flops 805306368 | bytes 6291456 | tf_op jit(solution)/shard_map/owner/pallas_call | solution.py:424
  145.0 2.2 late.1.turned_ref
  148.4 1.1 term.5
  150.8 3.1 %collective-permute-start.22 = (f32[384,256]{1,0:T(8,128)S(1)}, f32[384,256]{1,0:T(8,128)S(1)}, u32[]{:S(2)}, u32[]{:S(2)}) collective-permute-start(f32[384,256]{1,0:T(8,128)S(1)} %term.4), channel_id=1, source_target_pairs={{0,16},{1,17},{2,18},{3,19},{4,20},{5,21},{6,22},{7,23},{8,24},{9,... | collective-permute-start | bytes 1179656 | tf_op jit(solution)/shard_map/ppermute | solution.py:451
  154.4 2.7 %collective-permute-start.24 = (f32[384,256]{1,0:T(8,128)S(1)}, f32[384,256]{1,0:T(8,128)S(1)}, u32[]{:S(2)}, u32[]{:S(2)}) collective-permute-start(f32[384,256]{1,0:T(8,128)S(1)} %term.6), channel_id=1, source_target_pairs={{0,24},{1,25},{2,26},{3,27},{4,28},{5,29},{6,30},{7,31},{8,0},{9,1... | collective-permute-start | bytes 1179656 | tf_op jit(solution)/shard_map/ppermute | solution.py:451
  157.1 3.8 %inner.1 = (bf16[256,1024]{1,0:T(8,128)(2,1)S(1)}, f32[256,1024]{1,0:T(8,128)S(1)}, f32[256,1024]{1,0:T(8,128)S(1)}) custom-call(bf16[256,1024]{1,0:T(8,128)(2,1)S(1)} %copy-done.4, bf16[256,1024]{1,0:T(8,128)(2,1)S(1)} %copy-done.2, bf16[256,1024]{1,0:T(8,128)(2,1)S(1)} %copy-done.3, bf16[256,1024]{1,0:T(8,128)(2,1)S(1)} %copy-done.8, ...), custom_call_target="tpu_custom_call" | custom-call | flops 671088640 | bytes 6291456 | tf_op jit(solution)/shard_map/inner/pallas_call | solution.py:424
  161.0 4.2 %rows.1.refs_4_ = bf16[256,1024]{1,0:T(8,128)(2,1)} custom-call(bf16[256,1024]{1,0:T(8,128)(2,1)S(1)} %get-tuple-element.68.dq_ref, f32[256,1024]{1,0:T(8,128)S(1)} %get-tuple-element.69.dki_ref, f32[256,1024]{1,0:T(8,128)S(1)} %get-tuple-element.70.dvi_ref, bf16[256,1024]{1,0:T(8,128)(2,1)S(1)} %copy-done.2, bf16[256,1024]{1,0:T(8,128)(2,1)S(1)} %copy-done.3, ...), custom_call_target="tpu_custom_call" | custom-call | flops 1610612736 | bytes 8388608 | tf_op jit(solution)/shard_map/rows/pallas_call | solution.py:573
  166.3 4.1 %collective-permute-done.23.refs_1_ = f32[384,256]{1,0:T(8,128)S(1)} collective-permute-done((f32[384,256]{1,0:T(8,128)S(1)}, f32[384,256]{1,0:T(8,128)S(1)}, u32[]{:S(2)}, u32[]{:S(2)}) %collective-permute-start.23) | collective-permute-done | bytes 393248 | tf_op jit(solution)/shard_map/ppermute | solution.py:451
  171.2 1.6 collective-permute-start.25
  172.7 3.6 %collective-permute-start.26 = (f32[32,384]{1,0:T(8,128)S(1)}, f32[32,384]{1,0:T(8,128)S(1)}, u32[]{:S(2)}, u32[]{:S(2)}) collective-permute-start(f32[32,384]{1,0:T(8,128)S(1)} %get-tuple-element.101), channel_id=1, source_target_pairs={{0,2},{1,3},{2,4},{3,5},{4,6},{5,7},{6,0},{7,1},{8,10},{9,11},{10,... | collective-permute-start | bytes 147464 | tf_op jit(solution)/shard_map/ppermute | solution.py:448
  176.9 3.2 %collective-permute-start.28 = (f32[32,384]{1,0:T(8,128)S(1)}, f32[32,384]{1,0:T(8,128)S(1)}, u32[]{:S(2)}, u32[]{:S(2)}) collective-permute-start(f32[32,384]{1,0:T(8,128)S(1)} %get-tuple-element.103), channel_id=1, source_target_pairs={{0,4},{1,5},{2,6},{3,7},{4,0},{5,1},{6,2},{7,3},{8,12},{9,13},{10,... | collective-permute-start | bytes 147464 | tf_op jit(solution)/shard_map/ppermute | solution.py:448
  180.1 1.7 collective-permute-start.29
  181.9 2.4 %collective-permute-start.30 = (f32[32,384]{1,0:T(8,128)S(1)}, f32[32,384]{1,0:T(8,128)S(1)}, u32[]{:S(2)}, u32[]{:S(2)}) collective-permute-start(f32[32,384]{1,0:T(8,128)S(1)} %get-tuple-element.105), channel_id=1, source_target_pairs={{0,6},{1,7},{2,0},{3,1},{4,2},{5,3},{6,4},{7,5},{8,14},{9,15},{10,... | collective-permute-start | bytes 147464 | tf_op jit(solution)/shard_map/ppermute | solution.py:448
  184.3 2.6 %collective-permute-start.31 = (f32[32,384]{1,0:T(8,128)S(1)}, f32[32,384]{1,0:T(8,128)S(1)}, u32[]{:S(2)}, u32[]{:S(2)}) collective-permute-start(f32[32,384]{1,0:T(8,128)S(1)} %get-tuple-element.106), channel_id=1, source_target_pairs={{0,7},{1,0},{2,1},{3,2},{4,3},{5,4},{6,5},{7,6},{8,15},{9,8},{10,9... | collective-permute-start | bytes 147464 | tf_op jit(solution)/shard_map/ppermute | solution.py:448
  186.9 2.7 %collective-permute-done.29.refs_5_ = f32[32,384]{1,0:T(8,128)S(1)} collective-permute-done((f32[32,384]{1,0:T(8,128)S(1)}, f32[32,384]{1,0:T(8,128)S(1)}, u32[]{:S(2)}, u32[]{:S(2)}) %collective-permute-start.29) | collective-permute-done | bytes 49184 | tf_op jit(solution)/shard_map/ppermute | solution.py:448
  189.6 1.3 collective-permute-done.31.refs_7_
  191.0 1.2 collective-permute-done.32.other_ref
  192.2 3.2 %collective-permute-start.35 = (f32[2,32,384]{2,1,0:T(8,128)S(1)}, f32[2,32,384]{2,1,0:T(8,128)S(1)}, u32[]{:S(2)}, u32[]{:S(2)}) collective-permute-start(f32[2,32,384]{2,1,0:T(8,128)S(1)} %both.1.refs_0_), channel_id=1, source_target_pairs={{0,192},{32,224},{64,0},{96,32},{128,64},{160,96},{192,128},{224,1... | collective-permute-start | bytes 294920 | tf_op jit(solution)/shard_map/ppermute | solution.py:457
  196.4 3.5 %collective-permute-done.35.refs_3_ = f32[2,32,384]{2,1,0:T(8,128)S(1)} collective-permute-done((f32[2,32,384]{2,1,0:T(8,128)S(1)}, f32[2,32,384]{2,1,0:T(8,128)S(1)}, u32[]{:S(2)}, u32[]{:S(2)}) %collective-permute-start.35) | collective-permute-done | bytes 98336 | tf_op jit(solution)/shard_map/ppermute | solution.py:457
  199.9 2.7 %collective-permute-done.34.refs_2_ = f32[2,32,384]{2,1,0:T(8,128)S(1)} collective-permute-done((f32[2,32,384]{2,1,0:T(8,128)S(1)}, f32[2,32,384]{2,1,0:T(8,128)S(1)}, u32[]{:S(2)}, u32[]{:S(2)}) %collective-permute-start.34) | collective-permute-done | bytes 98336 | tf_op jit(solution)/shard_map/ppermute | solution.py:457
  203.5 16.8 %all_to_all.25.squares_ref = f32[32,8,128]{2,1,0:T(8,128)S(1)} all-to-all(f32[32,8,128]{2,1,0:T(8,128)S(1)} %square.1), channel_id=1, replica_groups=mesh['batch'=8,'seq'=32] {'seq'}, dimensions={0} | all-to-all | bytes 262144 | tf_op jit(solution)/shard_map/all_to_all | solution.py:607
  220.3 1.4 step.1
  (146 shorter events, 33.6 us)
Async XLA Ops:
  9.6 40.7 %copy-start.26 = (f32[128,1024]{1,0:T(8,128)S(1)}, f32[128,1024]{1,0:T(8,128)}, u32[]{:S(2)}) copy-start(f32[128,1024]{1,0:T(8,128)} %get-tuple-element.63.refs_1_) | copy-start | bytes 1572868
  9.6 40.7 %copy-start.2 = (bf16[256,1024]{1,0:T(8,128)(2,1)S(1)}, bf16[256,1024]{1,0:T(8,128)(2,1)}, u32[]{:S(2)}) copy-start(bf16[256,1024]{1,0:T(8,128)(2,1)} %get-tuple-element.56.k_ref) | copy-start | bytes 1572868
  9.6 40.6 %copy-start.3 = (bf16[256,1024]{1,0:T(8,128)(2,1)S(1)}, bf16[256,1024]{1,0:T(8,128)(2,1)}, u32[]{:S(2)}) copy-start(bf16[256,1024]{1,0:T(8,128)(2,1)} %get-tuple-element.57.v_ref) | copy-start | bytes 1572868
  9.7 40.6 %copy-start.4 = (bf16[256,1024]{1,0:T(8,128)(2,1)S(1)}, bf16[256,1024]{1,0:T(8,128)(2,1)}, u32[]{:S(2)}) copy-start(bf16[256,1024]{1,0:T(8,128)(2,1)} %get-tuple-element.55.q_ref) | copy-start | bytes 1572868
  9.7 40.6 %copy-start.9 = (f32[256,8]{1,0:T(8,128)S(1)}, f32[256,8]{1,0:T(8,128)}, u32[]{:S(2)}) copy-start(f32[256,8]{1,0:T(8,128)} %get-tuple-element.58.tall_ref) | copy-start | bytes 24580
  9.7 40.6 %copy-start.37 = (f32[8,256]{1,0:T(8,128)S(1)}, f32[8,256]{1,0:T(8,128)}, u32[]{:S(2)}) copy-start(f32[8,256]{1,0:T(8,128)} %get-tuple-element.59.flat_ref) | copy-start | bytes 24580
  9.7 31.8 %all-to-all-start = ((f32[32,40,128]{2,1,0:T(8,128)}), f32[32,40,128]{2,1,0:T(8,128)S(1)}, u32[]{:S(2)}, u32[]{:S(2)}) async-start(f32[32,40,128]{2,1,0:T(8,128)} %get-tuple-element.61), calls=%async_computation | async-start | bytes 1310720 | tf_op jit(solution)/shard_map/all_to_all | solution.py:507
  21.2 14.6 %collective-permute-start = (f32[128,1024]{1,0:T(8,128)}, f32[128,1024]{1,0:T(8,128)S(1)}, u32[]{:S(2)}, u32[]{:S(2)}) collective-permute-start(f32[128,1024]{1,0:T(8,128)} %get-tuple-element.62.refs_0_), channel_id=1, source_target_pairs={{0,64},{32,96},{64,128},{96,160},{128,192},{160,224},{192,0},{224,... | collective-permute-start | bytes 1572872 | tf_op jit(solution)/shard_map/ppermute | solution.py:457
  22.7 13.1 %collective-permute-start.1 = (f32[128,1024]{1,0:T(8,128)}, f32[128,1024]{1,0:T(8,128)S(1)}, u32[]{:S(2)}, u32[]{:S(2)}) collective-permute-start(f32[128,1024]{1,0:T(8,128)} %get-tuple-element.63.refs_1_), channel_id=1, source_target_pairs={{0,192},{32,224},{64,0},{96,32},{128,64},{160,96},{192,128},{224,1... | collective-permute-start | bytes 1572872 | tf_op jit(solution)/shard_map/ppermute | solution.py:457
  42.3 22.9 %all-to-all-start.1 = ((f32[32,32,128]{2,1,0:T(8,128)}), f32[32,32,128]{2,1,0:T(8,128)S(1)}, u32[]{:S(2)}, u32[]{:S(2)}) async-start(f32[32,32,128]{2,1,0:T(8,128)} %copy-done.31), calls=%async_computation.1 | async-start | bytes 1048576 | tf_op jit(solution)/shard_map/all_to_all | solution.py:511
  48.0 12.6 %collective-permute-start.3 = (f32[128,1024]{1,0:T(8,128)}, f32[128,1024]{1,0:T(8,128)}, u32[]{:S(2)}, u32[]{:S(2)}) collective-permute-start(f32[128,1024]{1,0:T(8,128)} %get-tuple-element.62.refs_0_), channel_id=1, source_target_pairs={{0,192},{32,224},{64,0},{96,32},{128,64},{160,96},{192,128},{224,1... | collective-permute-start | bytes 1572872 | tf_op jit(solution)/shard_map/ppermute | solution.py:457
  50.3 13.4 %collective-permute-start.2 = (f32[128,1024]{1,0:T(8,128)S(1)}, f32[128,1024]{1,0:T(8,128)S(1)}, u32[]{:S(2)}, u32[]{:S(2)}) collective-permute-start(f32[128,1024]{1,0:T(8,128)S(1)} %copy-done.26), channel_id=1, source_target_pairs={{0,64},{32,96},{64,128},{96,160},{128,192},{160,224},{192,0},{224,... | collective-permute-start | bytes 1572872 | tf_op jit(solution)/shard_map/ppermute | solution.py:457
  50.3 33.9 %copy-start.35 = (s32[2]{0:T(128)S(1)}, s32[2]{0:T(128)}, u32[]{:S(2)}) copy-start(s32[2]{0:T(128)} %pad_add_fusion.at_ref) | copy-start | bytes 28
  50.3 33.9 %copy-start.36 = (f32[1,8,256]{2,1,0:T(8,128)S(1)}, f32[1,8,256]{2,1,0:T(8,128)}, u32[]{:S(2)}) copy-start(f32[1,8,256]{2,1,0:T(8,128)} %param.5) | copy-start | bytes 24580
  71.1 26.6 %all-to-all-start.2 = ((f32[32,32,128]{2,1,0:T(8,128)}), f32[32,32,128]{2,1,0:T(8,128)S(1)}, u32[]{:S(2)}, u32[]{:S(2)}) async-start(f32[32,32,128]{2,1,0:T(8,128)} %copy-done.30), calls=%async_computation.2 | async-start | bytes 1048576 | tf_op jit(solution)/shard_map/all_to_all | solution.py:524
  80.9 15.4 %collective-permute-start.4 = (f32[128,1024]{1,0:T(8,128)}, f32[128,1024]{1,0:T(8,128)S(1)}, u32[]{:S(2)}, u32[]{:S(2)}) collective-permute-start(f32[128,1024]{1,0:T(8,128)} %copy-done.18), channel_id=1, source_target_pairs={{0,64},{32,96},{64,128},{96,160},{128,192},{160,224},{192,0},{224,... | collective-permute-start | bytes 1572872 | tf_op jit(solution)/shard_map/ppermute | solution.py:457
  81.0 15.9 %collective-permute-start.5 = (f32[128,1024]{1,0:T(8,128)}, f32[128,1024]{1,0:T(8,128)S(1)}, u32[]{:S(2)}, u32[]{:S(2)}) collective-permute-start(f32[128,1024]{1,0:T(8,128)} %copy-done.16), channel_id=1, source_target_pairs={{0,192},{32,224},{64,0},{96,32},{128,64},{160,96},{192,128},{224,1... | collective-permute-start | bytes 1572872 | tf_op jit(solution)/shard_map/ppermute | solution.py:457
  86.8 22.7 %collective-permute-start.14 = (f32[4,392,128]{2,1,0:T(8,128)}, f32[4,392,128]{2,1,0:T(8,128)}, u32[]{:S(2)}, u32[]{:S(2)}) collective-permute-start(f32[4,392,128]{2,1,0:T(8,128)} %get-tuple-element.82), channel_id=1, source_target_pairs={{0,32},{32,0},{64,96},{96,64},{128,160},{160,128},{192,224},{224,1... | collective-permute-start | bytes 2408456 | tf_op jit(solution)/shard_map/ppermute | solution.py:457
  86.8 21.7 %collective-permute-start.6 = (f32[128,1024]{1,0:T(8,128)}, f32[128,1024]{1,0:T(8,128)}, u32[]{:S(2)}, u32[]{:S(2)}) collective-permute-start(f32[128,1024]{1,0:T(8,128)} %get-tuple-element.62.refs_0_), channel_id=1, source_target_pairs={{0,32},{32,0},{64,96},{96,64},{128,160},{160,128},{192,224},{224,1... | collective-permute-start | bytes 1572872 | tf_op jit(solution)/shard_map/ppermute | solution.py:457
  87.3 21.7 %collective-permute-start.7 = (f32[128,1024]{1,0:T(8,128)}, f32[128,1024]{1,0:T(8,128)}, u32[]{:S(2)}, u32[]{:S(2)}) collective-permute-start(f32[128,1024]{1,0:T(8,128)} %get-tuple-element.63.refs_1_), channel_id=1, source_target_pairs={{0,32},{32,0},{64,96},{96,64},{128,160},{160,128},{192,224},{224,1... | collective-permute-start | bytes 1572872 | tf_op jit(solution)/shard_map/ppermute | solution.py:457
  96.3 12.8 %collective-permute-start.12 = (f32[128,1024]{1,0:T(8,128)}, f32[128,1024]{1,0:T(8,128)}, u32[]{:S(2)}, u32[]{:S(2)}) collective-permute-start(f32[128,1024]{1,0:T(8,128)} %collective-permute-done.3.refs_4_), channel_id=1, source_target_pairs={{0,32},{32,0},{64,96},{96,64},{128,160},{160,128},{192,224},{224,1... | collective-permute-start | bytes 1572872 | tf_op jit(solution)/shard_map/ppermute | solution.py:457
  98.5 27.7 %all-to-all-start.3 = ((f32[32,32,128]{2,1,0:T(8,128)}), f32[32,32,128]{2,1,0:T(8,128)S(1)}, u32[]{:S(2)}, u32[]{:S(2)}) async-start(f32[32,32,128]{2,1,0:T(8,128)} %copy-done.29), calls=%async_computation.3 | async-start | bytes 1048576 | tf_op jit(solution)/shard_map/all_to_all | solution.py:548
  108.3 5.4 %collective-permute-start.8 = (f32[128,1024]{1,0:T(8,128)}, f32[128,1024]{1,0:T(8,128)S(1)}, u32[]{:S(2)}, u32[]{:S(2)}) collective-permute-start(f32[128,1024]{1,0:T(8,128)} %copy-done.18), channel_id=1, source_target_pairs={{0,32},{32,0},{64,96},{96,64},{128,160},{160,128},{192,224},{224,1... | collective-permute-start | bytes 1572872 | tf_op jit(solution)/shard_map/ppermute | solution.py:457
  108.5 5.3 %collective-permute-start.9 = (f32[128,1024]{1,0:T(8,128)}, f32[128,1024]{1,0:T(8,128)S(1)}, u32[]{:S(2)}, u32[]{:S(2)}) collective-permute-start(f32[128,1024]{1,0:T(8,128)} %copy-done.20), channel_id=1, source_target_pairs={{0,32},{32,0},{64,96},{96,64},{128,160},{160,128},{192,224},{224,1... | collective-permute-start | bytes 1572872 | tf_op jit(solution)/shard_map/ppermute | solution.py:457
  108.9 6.3 %collective-permute-start.13 = (f32[128,1024]{1,0:T(8,128)}, f32[128,1024]{1,0:T(8,128)S(1)}, u32[]{:S(2)}, u32[]{:S(2)}) collective-permute-start(f32[128,1024]{1,0:T(8,128)} %copy-done.16), channel_id=1, source_target_pairs={{0,32},{32,0},{64,96},{96,64},{128,160},{160,128},{192,224},{224,1... | collective-permute-start | bytes 1572872 | tf_op jit(solution)/shard_map/ppermute | solution.py:457
  109.1 8.0 %collective-permute-start.10 = (f32[128,1024]{1,0:T(8,128)}, f32[128,1024]{1,0:T(8,128)S(1)}, u32[]{:S(2)}, u32[]{:S(2)}) collective-permute-start(f32[128,1024]{1,0:T(8,128)} %copy-done.22), channel_id=1, source_target_pairs={{0,32},{32,0},{64,96},{96,64},{128,160},{160,128},{192,224},{224,1... | collective-permute-start | bytes 1572872 | tf_op jit(solution)/shard_map/ppermute | solution.py:457
  109.5 7.6 %collective-permute-start.11 = (f32[128,1024]{1,0:T(8,128)}, f32[128,1024]{1,0:T(8,128)S(1)}, u32[]{:S(2)}, u32[]{:S(2)}) collective-permute-start(f32[128,1024]{1,0:T(8,128)} %copy-done.24), channel_id=1, source_target_pairs={{0,32},{32,0},{64,96},{96,64},{128,160},{160,128},{192,224},{224,1... | collective-permute-start | bytes 1572872 | tf_op jit(solution)/shard_map/ppermute | solution.py:457
  113.7 22.2 %collective-permute-start.15 = (f32[2,392,128]{2,1,0:T(8,128)}, f32[2,392,128]{2,1,0:T(8,128)}, u32[]{:S(2)}, u32[]{:S(2)}) collective-permute-start(f32[2,392,128]{2,1,0:T(8,128)} %get-tuple-element.84), channel_id=1, source_target_pairs={{0,64},{32,96},{64,128},{96,160},{128,192},{160,224},{192,0},{224,... | collective-permute-start | bytes 1204232 | tf_op jit(solution)/shard_map/ppermute | solution.py:457
  113.7 22.2 %collective-permute-start.16 = (f32[2,392,128]{2,1,0:T(8,128)}, f32[2,392,128]{2,1,0:T(8,128)}, u32[]{:S(2)}, u32[]{:S(2)}) collective-permute-start(f32[2,392,128]{2,1,0:T(8,128)} %get-tuple-element.85), channel_id=1, source_target_pairs={{0,128},{32,160},{64,192},{96,224},{128,0},{160,32},{192,64},{224,... | collective-permute-start | bytes 1204232 | tf_op jit(solution)/shard_map/ppermute | solution.py:457
  115.2 21.7 %collective-permute-start.17 = (f32[2,392,128]{2,1,0:T(8,128)}, f32[2,392,128]{2,1,0:T(8,128)}, u32[]{:S(2)}, u32[]{:S(2)}) collective-permute-start(f32[2,392,128]{2,1,0:T(8,128)} %get-tuple-element.86), channel_id=1, source_target_pairs={{0,192},{32,224},{64,0},{96,32},{128,64},{160,96},{192,128},{224,1... | collective-permute-start | bytes 1204232 | tf_op jit(solution)/shard_map/ppermute | solution.py:457
  126.8 1.6 collective-permute-start.18
  128.5 16.5 %collective-permute-start.19 = (f32[2,128,128]{2,1,0:T(8,128)S(1)}, f32[2,128,128]{2,1,0:T(8,128)S(1)}, u32[]{:S(2)}, u32[]{:S(2)}) collective-permute-start(f32[2,128,128]{2,1,0:T(8,128)S(1)} %get-tuple-element.94), channel_id=1, source_target_pairs={{0,64},{32,96},{64,128},{96,160},{128,192},{160,224},{192,0},{224,... | collective-permute-start | bytes 393224 | tf_op jit(solution)/shard_map/ppermute | solution.py:457
  129.2 15.8 %collective-permute-start.20 = (f32[2,128,128]{2,1,0:T(8,128)S(1)}, f32[2,128,128]{2,1,0:T(8,128)S(1)}, u32[]{:S(2)}, u32[]{:S(2)}) collective-permute-start(f32[2,128,128]{2,1,0:T(8,128)S(1)} %get-tuple-element.95), channel_id=1, source_target_pairs={{0,128},{32,160},{64,192},{96,224},{128,0},{160,32},{192,64},{224,... | collective-permute-start | bytes 393224 | tf_op jit(solution)/shard_map/ppermute | solution.py:457
  136.0 9.1 %collective-permute-start.21 = (f32[2,128,128]{2,1,0:T(8,128)S(1)}, f32[2,128,128]{2,1,0:T(8,128)S(1)}, u32[]{:S(2)}, u32[]{:S(2)}) collective-permute-start(f32[2,128,128]{2,1,0:T(8,128)S(1)} %get-tuple-element.96), channel_id=1, source_target_pairs={{0,192},{32,224},{64,0},{96,32},{128,64},{160,96},{192,128},{224,1... | collective-permute-start | bytes 393224 | tf_op jit(solution)/shard_map/ppermute | solution.py:457
  150.8 15.5 %collective-permute-start.22 = (f32[384,256]{1,0:T(8,128)S(1)}, f32[384,256]{1,0:T(8,128)S(1)}, u32[]{:S(2)}, u32[]{:S(2)}) collective-permute-start(f32[384,256]{1,0:T(8,128)S(1)} %term.4), channel_id=1, source_target_pairs={{0,16},{1,17},{2,18},{3,19},{4,20},{5,21},{6,22},{7,23},{8,24},{9,... | collective-permute-start | bytes 1179656 | tf_op jit(solution)/shard_map/ppermute | solution.py:451
  153.9 16.5 %collective-permute-start.23 = (f32[384,256]{1,0:T(8,128)S(1)}, f32[384,256]{1,0:T(8,128)S(1)}, u32[]{:S(2)}, u32[]{:S(2)}) collective-permute-start(f32[384,256]{1,0:T(8,128)S(1)} %term.5), channel_id=1, source_target_pairs={{0,8},{1,9},{2,10},{3,11},{4,12},{5,13},{6,14},{7,15},{8,16},{9,17... | collective-permute-start | bytes 1179656 | tf_op jit(solution)/shard_map/ppermute | solution.py:451
  154.4 16.0 %collective-permute-start.24 = (f32[384,256]{1,0:T(8,128)S(1)}, f32[384,256]{1,0:T(8,128)S(1)}, u32[]{:S(2)}, u32[]{:S(2)}) collective-permute-start(f32[384,256]{1,0:T(8,128)S(1)} %term.6), channel_id=1, source_target_pairs={{0,24},{1,25},{2,26},{3,27},{4,28},{5,29},{6,30},{7,31},{8,0},{9,1... | collective-permute-start | bytes 1179656 | tf_op jit(solution)/shard_map/ppermute | solution.py:451
  171.2 10.7 %collective-permute-start.25 = (f32[32,384]{1,0:T(8,128)S(1)}, f32[32,384]{1,0:T(8,128)S(1)}, u32[]{:S(2)}, u32[]{:S(2)}) collective-permute-start(f32[32,384]{1,0:T(8,128)S(1)} %get-tuple-element.100), channel_id=1, source_target_pairs={{0,1},{1,2},{2,3},{3,4},{4,5},{5,6},{6,7},{7,0},{8,9},{9,10},{10,1... | collective-permute-start | bytes 147464 | tf_op jit(solution)/shard_map/ppermute | solution.py:448
  172.7 11.6 %collective-permute-start.26 = (f32[32,384]{1,0:T(8,128)S(1)}, f32[32,384]{1,0:T(8,128)S(1)}, u32[]{:S(2)}, u32[]{:S(2)}) collective-permute-start(f32[32,384]{1,0:T(8,128)S(1)} %get-tuple-element.101), channel_id=1, source_target_pairs={{0,2},{1,3},{2,4},{3,5},{4,6},{5,7},{6,0},{7,1},{8,10},{9,11},{10,... | collective-permute-start | bytes 147464 | tf_op jit(solution)/shard_map/ppermute | solution.py:448
  176.3 10.6 %collective-permute-start.27 = (f32[32,384]{1,0:T(8,128)S(1)}, f32[32,384]{1,0:T(8,128)S(1)}, u32[]{:S(2)}, u32[]{:S(2)}) collective-permute-start(f32[32,384]{1,0:T(8,128)S(1)} %get-tuple-element.102), channel_id=1, source_target_pairs={{0,3},{1,4},{2,5},{3,6},{4,7},{5,0},{6,1},{7,2},{8,11},{9,12},{10,... | collective-permute-start | bytes 147464 | tf_op jit(solution)/shard_map/ppermute | solution.py:448
  176.9 10.0 %collective-permute-start.28 = (f32[32,384]{1,0:T(8,128)S(1)}, f32[32,384]{1,0:T(8,128)S(1)}, u32[]{:S(2)}, u32[]{:S(2)}) collective-permute-start(f32[32,384]{1,0:T(8,128)S(1)} %get-tuple-element.103), channel_id=1, source_target_pairs={{0,4},{1,5},{2,6},{3,7},{4,0},{5,1},{6,2},{7,3},{8,12},{9,13},{10,... | collective-permute-start | bytes 147464 | tf_op jit(solution)/shard_map/ppermute | solution.py:448
  180.1 9.5 %collective-permute-start.29 = (f32[32,384]{1,0:T(8,128)S(1)}, f32[32,384]{1,0:T(8,128)S(1)}, u32[]{:S(2)}, u32[]{:S(2)}) collective-permute-start(f32[32,384]{1,0:T(8,128)S(1)} %get-tuple-element.104), channel_id=1, source_target_pairs={{0,5},{1,6},{2,7},{3,0},{4,1},{5,2},{6,3},{7,4},{8,13},{9,14},{10,... | collective-permute-start | bytes 147464 | tf_op jit(solution)/shard_map/ppermute | solution.py:448
  181.9 7.8 %collective-permute-start.30 = (f32[32,384]{1,0:T(8,128)S(1)}, f32[32,384]{1,0:T(8,128)S(1)}, u32[]{:S(2)}, u32[]{:S(2)}) collective-permute-start(f32[32,384]{1,0:T(8,128)S(1)} %get-tuple-element.105), channel_id=1, source_target_pairs={{0,6},{1,7},{2,0},{3,1},{4,2},{5,3},{6,4},{7,5},{8,14},{9,15},{10,... | collective-permute-start | bytes 147464 | tf_op jit(solution)/shard_map/ppermute | solution.py:448
  184.3 6.6 %collective-permute-start.31 = (f32[32,384]{1,0:T(8,128)S(1)}, f32[32,384]{1,0:T(8,128)S(1)}, u32[]{:S(2)}, u32[]{:S(2)}) collective-permute-start(f32[32,384]{1,0:T(8,128)S(1)} %get-tuple-element.106), channel_id=1, source_target_pairs={{0,7},{1,0},{2,1},{3,2},{4,3},{5,4},{6,5},{7,6},{8,15},{9,8},{10,9... | collective-permute-start | bytes 147464 | tf_op jit(solution)/shard_map/ppermute | solution.py:448
  190.9 1.3 collective-permute-start.32
  192.2 7.7 %collective-permute-start.35 = (f32[2,32,384]{2,1,0:T(8,128)S(1)}, f32[2,32,384]{2,1,0:T(8,128)S(1)}, u32[]{:S(2)}, u32[]{:S(2)}) collective-permute-start(f32[2,32,384]{2,1,0:T(8,128)S(1)} %both.1.refs_0_), channel_id=1, source_target_pairs={{0,192},{32,224},{64,0},{96,32},{128,64},{160,96},{192,128},{224,1... | collective-permute-start | bytes 294920 | tf_op jit(solution)/shard_map/ppermute | solution.py:457
  195.5 7.1 %collective-permute-start.34 = (f32[2,32,384]{2,1,0:T(8,128)S(1)}, f32[2,32,384]{2,1,0:T(8,128)S(1)}, u32[]{:S(2)}, u32[]{:S(2)}) collective-permute-start(f32[2,32,384]{2,1,0:T(8,128)S(1)} %both.1.refs_0_), channel_id=1, source_target_pairs={{0,128},{32,160},{64,192},{96,224},{128,0},{160,32},{192,64},{224,... | collective-permute-start | bytes 294920 | tf_op jit(solution)/shard_map/ppermute | solution.py:457
  195.8 7.6 %collective-permute-start.33 = (f32[2,32,384]{2,1,0:T(8,128)S(1)}, f32[2,32,384]{2,1,0:T(8,128)S(1)}, u32[]{:S(2)}, u32[]{:S(2)}) collective-permute-start(f32[2,32,384]{2,1,0:T(8,128)S(1)} %both.1.refs_0_), channel_id=1, source_target_pairs={{0,64},{32,96},{64,128},{96,160},{128,192},{160,224},{192,0},{224,... | collective-permute-start | bytes 294920 | tf_op jit(solution)/shard_map/ppermute | solution.py:457
  (34 other events, 94.5 us)
where the time goes:
time: 223 us; the launch traced here: 222 us
  starting transfers between devices  80.5 us (36%)
  Pallas kernels  51.2 us (23%)
  waiting for transfers between devices  48.6 us (22%)
  local copies, waits for them, and re-layouts  22.2 us (10%)
  blocking collectives  16.8 us (8%)
    pallas_call x22, Pallas kernels, kernel(): pl.pallas_call(body, in_specs=[pl.BlockSpec(memory_space=space(place)) fo...  38.7 us
    ppermute x26, waiting for transfers between devices, along_users(): return lax.ppermute(array, 'batch', pairs_of)  35.3 us
    unnamed x84, local copies, waits for them, and re-layouts  22.2 us
    ppermute x26, starting transfers between devices, along_users(): return lax.ppermute(array, 'batch', pairs_of)  21.6 us
    all_to_all x2, starting transfers between devices, on_device(): got = lax.all_to_all(sums, 'seq', 0, 0)  21.3 us
    all_to_all x1, blocking collectives, on_device(): squares = lax.all_to_all(squares, 'seq', 0, 0)  16.8 us
    ppermute x7, starting transfers between devices, along_line(): return lax.ppermute(array, 'seq', pairs_of)  15.8 us
    all_to_all x1, starting transfers between devices, on_device(): back = lax.all_to_all(entered, 'seq', 0, 0).reshape(heads, size, size)  9.8 us
  transfers between devices with their start and end apart: 40, of which 16 were waited for; matrix products, arithmetic and copies ran while one was open for 0% of the time, Pallas kernels for 14%

commit v1 on v0

--- a/solution.py
+++ b/solution.py
@@ -533,7 +533,7 @@
         return kernel(
             recall_kernel,
             [shape((count, length, width), half), shape((count, length, 3 * size), half), shape((EXTRA, size))],
-            6 * length * width * size * count, 8 << 20, name, False, after=2, limit=50,
+            6 * length * width * size * count, 8 << 20, name, False, after=2, limit=58,
             scratch_shapes=[pltpu.VMEM((count, length, width), flt), pltpu.SemaphoreType.DMA((2 * count,))],
         )(weight_columns, after, *wide)
 

time: 223 us -> 221 us (level)
  local copies, waits for them, and re-layouts: 22.2 us -> 15.2 us
  Pallas kernels: 51.2 us -> 53.6 us
    unnamed x84 -> x78, local copies, waits for them, and re-layouts: 22.2 us -> 15.2 us
    pallas_call x22, Pallas kernels: 38.7 us -> 41 us  [kernel(): pl.pallas_call(body, in_specs=[pl.BlockSpec(memory_space=space(place)) fo...]
  transfers between devices with their start and end apart: 40 -> 40, of which waited for: 16 -> 17; matrix products, arithmetic and copies ran while one was open for 0% -> 1% of each run, Pallas kernels for 14% -> 15%
where the time goes in v1:
time: 221 us; the launch traced here: 220 us
  starting transfers between devices  80.7 us (37%)
  Pallas kernels  53.6 us (24%)
  waiting for transfers between devices  50 us (23%)
  blocking collectives  16.7 us (8%)
  local copies, waits for them, and re-layouts  15.2 us (7%)
  other arithmetic  2.62 us (1%)
    pallas_call x22, Pallas kernels, kernel(): pl.pallas_call(body, in_specs=[pl.BlockSpec(memory_space=space(place)) fo...  41 us
    ppermute x26, waiting for transfers between devices, along_users(): return lax.ppermute(array, 'batch', pairs_of)  34.7 us
    ppermute x26, starting transfers between devices, along_users(): return lax.ppermute(array, 'batch', pairs_of)  23.2 us
    all_to_all x2, starting transfers between devices, on_device(): got = lax.all_to_all(sums, 'seq', 0, 0)  21.3 us
    all_to_all x1, blocking collectives, on_device(): squares = lax.all_to_all(squares, 'seq', 0, 0)  16.7 us
    ppermute x7, starting transfers between devices, along_line(): return lax.ppermute(array, 'seq', pairs_of)  15.8 us
    unnamed x78, local copies, waits for them, and re-layouts  15.2 us
    all_to_all x1, starting transfers between devices, on_device(): back = lax.all_to_all(entered, 'seq', 0, 0).reshape(heads, size, size)  8.4 us
  transfers between devices with their start and end apart: 40, of which 17 were waited for; matrix products, arithmetic and copies ran while one was open for 1% of the time, Pallas kernels for 15%

profile of v1, /device:TPU:32, one launch (start us, length us, event | category | flops | bytes accessed | tf_op | source)
XLA Modules:
  0.0 220.0 jit_solution(6584563669801748274)
XLA Ops:
  1.3 8.4 %project.1 = (bf16[256,1024]{1,0:T(8,128)(2,1)}, bf16[256,1024]{1,0:T(8,128)(2,1)}, bf16[256,1024]{1,0:T(8,128)(2,1)}, f32[256,8]{1,0:T(8,128)}, f32[8,256]{1,0:...) custom-call(s32[2]{0:T(128)} %pad_add_fusion.at_ref, ...), custom_call_target="tpu_custom_call" | custom-call | flops 1610612736 | bytes 8388608 | tf_op jit(solution)/shard_map/project/pallas_call | solution.py:480
  9.7 11.5 %all-to-all-start = ((f32[32,40,128]{2,1,0:T(8,128)}), f32[32,40,128]{2,1,0:T(8,128)S(1)}, u32[]{:S(2)}, u32[]{:S(2)}) async-start(f32[32,40,128]{2,1,0:T(8,128)} %get-tuple-element.61), calls=%async_computation | async-start | bytes 1310720 | tf_op jit(solution)/shard_map/all_to_all | solution.py:507
  21.2 1.5 collective-permute-start
  22.7 1.8 collective-permute-start.1
  24.5 11.3 %collective-permute-done.refs_2_ = f32[128,1024]{1,0:T(8,128)S(1)} collective-permute-done((f32[128,1024]{1,0:T(8,128)}, f32[128,1024]{1,0:T(8,128)S(1)}, u32[]{:S(2)}, u32[]{:S(2)}) %collective-permute-start) | collective-permute-done | bytes 524320 | tf_op jit(solution)/shard_map/ppermute | solution.py:457
  37.3 4.2 %all-to-all-done.got_ref = f32[32,40,128]{2,1,0:T(8,128)S(1)} async-done(((f32[32,40,128]{2,1,0:T(8,128)}), f32[32,40,128]{2,1,0:T(8,128)S(1)}, u32[]{:S(2)}, u32[]{:S(2)}) %all-to-all-start) | async-done | bytes 655392 | tf_op jit(solution)/shard_map/all_to_all | solution.py:507
  42.4 5.8 %all-to-all-start.1 = ((f32[32,32,128]{2,1,0:T(8,128)}), f32[32,32,128]{2,1,0:T(8,128)S(1)}, u32[]{:S(2)}, u32[]{:S(2)}) async-start(f32[32,32,128]{2,1,0:T(8,128)} %get-tuple-element.64), calls=%async_computation.1 | async-start | bytes 1048576 | tf_op jit(solution)/shard_map/all_to_all | solution.py:511
  48.1 2.2 %collective-permute-start.3 = (f32[128,1024]{1,0:T(8,128)}, f32[128,1024]{1,0:T(8,128)}, u32[]{:S(2)}, u32[]{:S(2)}) collective-permute-start(f32[128,1024]{1,0:T(8,128)} %get-tuple-element.62.refs_0_), channel_id=1, source_target_pairs={{0,192},{32,224},{64,0},{96,32},{128,64},{160,96},{192,128},{224,1... | collective-permute-start | bytes 1572872 | tf_op jit(solution)/shard_map/ppermute | solution.py:457
  50.4 2.7 %weights.1 = (bf16[8,256,256]{2,1,0:T(8,128)(2,1)S(1)}, f32[256,1024]{1,0:T(8,128)S(1)}) custom-call(bf16[256,1024]{1,0:T(8,128)(2,1)S(1)} %copy-done.4, bf16[256,1024]{1,0:T(8,128)(2,1)S(1)} %copy-done.2, bf16[256,1024]{1,0:T(8,128)(2,1)S(1)} %copy-done.3, f32[256,8]{1,0:T(8,128)S(1)} %copy-done.10, f32[8,256]{1,0:T(8,128)S(1)} %copy-done.24), custom_call_target="tpu_custom_call" | custom-call | flops 268435456 | bytes 5242880 | tf_op jit(solution)/shard_map/weights/pallas_call | solution.py:424
  55.1 5.6 %collective-permute-done.3.refs_4_ = f32[128,1024]{1,0:T(8,128)} collective-permute-done((f32[128,1024]{1,0:T(8,128)}, f32[128,1024]{1,0:T(8,128)}, u32[]{:S(2)}, u32[]{:S(2)}) %collective-permute-start.3) | collective-permute-done | bytes 524320 | tf_op jit(solution)/shard_map/ppermute | solution.py:457
  60.7 3.3 %collective-permute-done.2.refs_3_ = f32[128,1024]{1,0:T(8,128)S(1)} collective-permute-done((f32[128,1024]{1,0:T(8,128)}, f32[128,1024]{1,0:T(8,128)S(1)}, u32[]{:S(2)}, u32[]{:S(2)}) %collective-permute-start.2) | collective-permute-done | bytes 524320 | tf_op jit(solution)/shard_map/ppermute | solution.py:457
  65.5 1.2 copy-done.12
  67.8 2.8 %mix.1 = (bf16[256,1024]{1,0:T(8,128)(2,1)}, bf16[256,1024]{1,0:T(8,128)(2,1)S(1)}, f32[32,32,128]{2,1,0:T(8,128)S(1)}) custom-call(bf16[256,1024]{1,0:T(8,128)(2,1)S(1)} %copy-done.4, f32[256,1024]{1,0:T(8,128)S(1)} %copy-done.12, bf16[256,1024]{1,0:T(8,128)(2,1)S(1)} %bitcast.16, f32[256,8]{1,0:T(8,128)S(1)} %copy-done.10, f32[8,128,128]{2,1,0:T(8,128)S(1)} %bitcast.11, ...), custom_call_target="tpu_custom_call" | custom-call | flops 134217728 | bytes 5242880 | tf_op jit(solution)/shard_map/mix/pallas_call | solution.py:424
  71.4 9.8 %all-to-all-start.2 = ((f32[32,32,128]{2,1,0:T(8,128)}), f32[32,32,128]{2,1,0:T(8,128)S(1)}, u32[]{:S(2)}, u32[]{:S(2)}) async-start(f32[32,32,128]{2,1,0:T(8,128)} %copy-done.18), calls=%async_computation.2 | async-start | bytes 1048576 | tf_op jit(solution)/shard_map/all_to_all | solution.py:524
  81.3 3.2 %collective-permute-start.5 = (f32[128,1024]{1,0:T(8,128)}, f32[128,1024]{1,0:T(8,128)S(1)}, u32[]{:S(2)}, u32[]{:S(2)}) collective-permute-start(f32[128,1024]{1,0:T(8,128)} %copy-done.27), channel_id=1, source_target_pairs={{0,192},{32,224},{64,0},{96,32},{128,64},{160,96},{192,128},{224,1... | collective-permute-start | bytes 1572872 | tf_op jit(solution)/shard_map/ppermute | solution.py:457
  84.5 1.6 pack.1
  87.5 4.9 %recall.1 = (bf16[3,256,1024]{2,1,0:T(8,128)(2,1)}, bf16[3,256,384]{2,1,0:T(8,128)(2,1)}, f32[8,128]{1,0:T(8,128)}) custom-call(bf16[1024,384]{1,0:T(8,128)(2,1)} %get-tuple-element.73.weight_ref, f32[8,128]{1,0:T(8,128)} %get-tuple-element.107.after_ref, f32[128,1024]{1,0:T(8,128)} %get-tuple-element.62.refs_0_, f32[128,1024]{1,0:T(8,128)} %get-tuple-element.63.refs_1_, ...), custom_call_target="tpu_custom_call" | custom-call | flops 603979776 | bytes 8388608 | tf_op jit(solution)/shard_map/recall/pallas_call | solution.py:424
  95.0 1.4 all-to-all-done.2.got_ref
  97.3 8.4 %all-to-all-start.3 = ((f32[32,32,128]{2,1,0:T(8,128)}), f32[32,32,128]{2,1,0:T(8,128)S(1)}, u32[]{:S(2)}, u32[]{:S(2)}) async-start(f32[32,32,128]{2,1,0:T(8,128)} %copy-done.17), calls=%async_computation.3 | async-start | bytes 1048576 | tf_op jit(solution)/shard_map/all_to_all | solution.py:548
  108.3 2.2 pair.2
  111.2 4.2 %collective-permute-start.16 = (f32[2,392,128]{2,1,0:T(8,128)}, f32[2,392,128]{2,1,0:T(8,128)}, u32[]{:S(2)}, u32[]{:S(2)}) collective-permute-start(f32[2,392,128]{2,1,0:T(8,128)} %get-tuple-element.85), channel_id=1, source_target_pairs={{0,128},{32,160},{64,192},{96,224},{128,0},{160,32},{192,64},{224,... | collective-permute-start | bytes 1204232 | tf_op jit(solution)/shard_map/ppermute | solution.py:457
  116.6 6.3 %recall_rest.1 = (bf16[5,256,1024]{2,1,0:T(8,128)(2,1)}, bf16[5,256,384]{2,1,0:T(8,128)(2,1)}, f32[8,128]{1,0:T(8,128)}) custom-call(bf16[1024,384]{1,0:T(8,128)(2,1)} %get-tuple-element.73.weight_ref, f32[8,128]{1,0:T(8,128)} %copy-done.25, f32[128,1024]{1,0:T(8,128)} %copy-done.30, f32[128,1024]{1,0:T(8,128)} %copy-done.31, ...), custom_call_target="tpu_custom_call" | custom-call | flops 1006632960 | bytes 8388608 | tf_op jit(solution)/shard_map/recall_rest/pallas_call | solution.py:424
  125.3 1.5 collective-permute-done.18.came_ref
  128.0 2.5 %collective-permute-start.21 = (f32[2,128,128]{2,1,0:T(8,128)S(1)}, f32[2,128,128]{2,1,0:T(8,128)S(1)}, u32[]{:S(2)}, u32[]{:S(2)}) collective-permute-start(f32[2,128,128]{2,1,0:T(8,128)S(1)} %get-tuple-element.96), channel_id=1, source_target_pairs={{0,192},{32,224},{64,0},{96,32},{128,64},{160,96},{192,128},{224,1... | collective-permute-start | bytes 393224 | tf_op jit(solution)/shard_map/ppermute | solution.py:457
  130.5 3.9 %collective-permute-done.16.refs_2_ = f32[2,392,128]{2,1,0:T(8,128)} collective-permute-done((f32[2,392,128]{2,1,0:T(8,128)}, f32[2,392,128]{2,1,0:T(8,128)}, u32[]{:S(2)}, u32[]{:S(2)}) %collective-permute-start.16) | collective-permute-done | bytes 401440 | tf_op jit(solution)/shard_map/ppermute | solution.py:457
  134.5 1.2 copy-done.5
  136.7 5.9 %owner.1 = (f32[256,8]{1,0:T(8,128)S(1)}, bf16[128,2048]{1,0:T(8,128)(2,1)S(1)}, f32[8,256,128]{2,1,0:T(8,128)S(1)}, f32[8,256,128]{2,1,0:T(8,128)S(1)}) custom-call(bf16[3,256,384]{2,1,0:T(8,128)(2,1)S(1)} %copy-done.6, bf16[5,256,384]{2,1,0:T(8,128)(2,1)S(1)} %copy-done.5, f32[2,392,128]{2,1,0:T(8,128)S(1)} %copy-done.21, ...), custom_call_target="tpu_custom_call" | custom-call | flops 805306368 | bytes 6291456 | tf_op jit(solution)/shard_map/owner/pallas_call | solution.py:424
  142.7 2.2 %late.1.turned_ref = bf16[384,2048]{1,0:T(8,128)(2,1)S(1)} custom-call(bf16[3,256,384]{2,1,0:T(8,128)(2,1)S(1)} %copy-done.6, bf16[5,256,384]{2,1,0:T(8,128)(2,1)S(1)} %copy-done.5, f32[8,256,128]{2,1,0:T(8,128)S(1)} %get-tuple-element.87.dk_ref, f32[8,256,128]{2,1,0:T(8,128)S(1)} %get-tuple-element.88.dv_ref, f32[256,8]{1,0:T(8,128)S(1)} %get-tuple-element.89.tall_ref, ...), custom_call_target="tpu_custom_call" | custom-call | flops 134217728 | bytes 4194304 | tf_op jit(solution)/shard_map/late/pallas_call | solution.py:424
  146.1 1.1 term.5
  148.4 3.1 %collective-permute-start.22 = (f32[384,256]{1,0:T(8,128)S(1)}, f32[384,256]{1,0:T(8,128)S(1)}, u32[]{:S(2)}, u32[]{:S(2)}) collective-permute-start(f32[384,256]{1,0:T(8,128)S(1)} %term.4), channel_id=1, source_target_pairs={{0,16},{1,17},{2,18},{3,19},{4,20},{5,21},{6,22},{7,23},{8,24},{9,... | collective-permute-start | bytes 1179656 | tf_op jit(solution)/shard_map/ppermute | solution.py:451
  152.1 2.6 %collective-permute-start.24 = (f32[384,256]{1,0:T(8,128)S(1)}, f32[384,256]{1,0:T(8,128)S(1)}, u32[]{:S(2)}, u32[]{:S(2)}) collective-permute-start(f32[384,256]{1,0:T(8,128)S(1)} %term.6), channel_id=1, source_target_pairs={{0,24},{1,25},{2,26},{3,27},{4,28},{5,29},{6,30},{7,31},{8,0},{9,1... | collective-permute-start | bytes 1179656 | tf_op jit(solution)/shard_map/ppermute | solution.py:451
  154.8 3.8 %inner.1 = (bf16[256,1024]{1,0:T(8,128)(2,1)S(1)}, f32[256,1024]{1,0:T(8,128)S(1)}, f32[256,1024]{1,0:T(8,128)S(1)}) custom-call(bf16[256,1024]{1,0:T(8,128)(2,1)S(1)} %copy-done.4, bf16[256,1024]{1,0:T(8,128)(2,1)S(1)} %copy-done.2, bf16[256,1024]{1,0:T(8,128)(2,1)S(1)} %copy-done.3, bf16[256,1024]{1,0:T(8,128)(2,1)S(1)} %copy-done.9, ...), custom_call_target="tpu_custom_call" | custom-call | flops 671088640 | bytes 6291456 | tf_op jit(solution)/shard_map/inner/pallas_call | solution.py:424
  158.6 4.2 %rows.1.refs_4_ = bf16[256,1024]{1,0:T(8,128)(2,1)} custom-call(bf16[256,1024]{1,0:T(8,128)(2,1)S(1)} %get-tuple-element.68.dq_ref, f32[256,1024]{1,0:T(8,128)S(1)} %get-tuple-element.69.dki_ref, f32[256,1024]{1,0:T(8,128)S(1)} %get-tuple-element.70.dvi_ref, bf16[256,1024]{1,0:T(8,128)(2,1)S(1)} %copy-done.2, bf16[256,1024]{1,0:T(8,128)(2,1)S(1)} %copy-done.3, ...), custom_call_target="tpu_custom_call" | custom-call | flops 1610612736 | bytes 8388608 | tf_op jit(solution)/shard_map/rows/pallas_call | solution.py:573
  164.0 4.6 %collective-permute-done.23.refs_1_ = f32[384,256]{1,0:T(8,128)S(1)} collective-permute-done((f32[384,256]{1,0:T(8,128)S(1)}, f32[384,256]{1,0:T(8,128)S(1)}, u32[]{:S(2)}, u32[]{:S(2)}) %collective-permute-start.23) | collective-permute-done | bytes 393248 | tf_op jit(solution)/shard_map/ppermute | solution.py:451
  169.5 1.5 collective-permute-start.25
  171.0 3.6 %collective-permute-start.26 = (f32[32,384]{1,0:T(8,128)S(1)}, f32[32,384]{1,0:T(8,128)S(1)}, u32[]{:S(2)}, u32[]{:S(2)}) collective-permute-start(f32[32,384]{1,0:T(8,128)S(1)} %get-tuple-element.101), channel_id=1, source_target_pairs={{0,2},{1,3},{2,4},{3,5},{4,6},{5,7},{6,0},{7,1},{8,10},{9,11},{10,... | collective-permute-start | bytes 147464 | tf_op jit(solution)/shard_map/ppermute | solution.py:448
  175.2 3.2 %collective-permute-start.28 = (f32[32,384]{1,0:T(8,128)S(1)}, f32[32,384]{1,0:T(8,128)S(1)}, u32[]{:S(2)}, u32[]{:S(2)}) collective-permute-start(f32[32,384]{1,0:T(8,128)S(1)} %get-tuple-element.103), channel_id=1, source_target_pairs={{0,4},{1,5},{2,6},{3,7},{4,0},{5,1},{6,2},{7,3},{8,12},{9,13},{10,... | collective-permute-start | bytes 147464 | tf_op jit(solution)/shard_map/ppermute | solution.py:448
  178.5 1.7 collective-permute-start.29
  180.2 2.4 %collective-permute-start.30 = (f32[32,384]{1,0:T(8,128)S(1)}, f32[32,384]{1,0:T(8,128)S(1)}, u32[]{:S(2)}, u32[]{:S(2)}) collective-permute-start(f32[32,384]{1,0:T(8,128)S(1)} %get-tuple-element.105), channel_id=1, source_target_pairs={{0,6},{1,7},{2,0},{3,1},{4,2},{5,3},{6,4},{7,5},{8,14},{9,15},{10,... | collective-permute-start | bytes 147464 | tf_op jit(solution)/shard_map/ppermute | solution.py:448
  182.6 2.7 %collective-permute-start.31 = (f32[32,384]{1,0:T(8,128)S(1)}, f32[32,384]{1,0:T(8,128)S(1)}, u32[]{:S(2)}, u32[]{:S(2)}) collective-permute-start(f32[32,384]{1,0:T(8,128)S(1)} %get-tuple-element.106), channel_id=1, source_target_pairs={{0,7},{1,0},{2,1},{3,2},{4,3},{5,4},{6,5},{7,6},{8,15},{9,8},{10,9... | collective-permute-start | bytes 147464 | tf_op jit(solution)/shard_map/ppermute | solution.py:448
  185.3 2.6 %collective-permute-done.29.refs_5_ = f32[32,384]{1,0:T(8,128)S(1)} collective-permute-done((f32[32,384]{1,0:T(8,128)S(1)}, f32[32,384]{1,0:T(8,128)S(1)}, u32[]{:S(2)}, u32[]{:S(2)}) %collective-permute-start.29) | collective-permute-done | bytes 49184 | tf_op jit(solution)/shard_map/ppermute | solution.py:448
  187.9 1.4 collective-permute-done.31.refs_7_
  189.4 1.2 collective-permute-done.32.other_ref
  190.6 3.3 %collective-permute-start.35 = (f32[2,32,384]{2,1,0:T(8,128)S(1)}, f32[2,32,384]{2,1,0:T(8,128)S(1)}, u32[]{:S(2)}, u32[]{:S(2)}) collective-permute-start(f32[2,32,384]{2,1,0:T(8,128)S(1)} %both.1.refs_0_), channel_id=1, source_target_pairs={{0,192},{32,224},{64,0},{96,32},{128,64},{160,96},{192,128},{224,1... | collective-permute-start | bytes 294920 | tf_op jit(solution)/shard_map/ppermute | solution.py:457
  194.9 3.5 %collective-permute-done.35.refs_3_ = f32[2,32,384]{2,1,0:T(8,128)S(1)} collective-permute-done((f32[2,32,384]{2,1,0:T(8,128)S(1)}, f32[2,32,384]{2,1,0:T(8,128)S(1)}, u32[]{:S(2)}, u32[]{:S(2)}) %collective-permute-start.35) | collective-permute-done | bytes 98336 | tf_op jit(solution)/shard_map/ppermute | solution.py:457
  198.4 2.7 %collective-permute-done.34.refs_2_ = f32[2,32,384]{2,1,0:T(8,128)S(1)} collective-permute-done((f32[2,32,384]{2,1,0:T(8,128)S(1)}, f32[2,32,384]{2,1,0:T(8,128)S(1)}, u32[]{:S(2)}, u32[]{:S(2)}) %collective-permute-start.34) | collective-permute-done | bytes 98336 | tf_op jit(solution)/shard_map/ppermute | solution.py:457
  201.8 16.7 %all_to_all.25.squares_ref = f32[32,8,128]{2,1,0:T(8,128)S(1)} all-to-all(f32[32,8,128]{2,1,0:T(8,128)S(1)} %square.1), channel_id=1, replica_groups=mesh['batch'=8,'seq'=32] {'seq'}, dimensions={0} | all-to-all | bytes 262144 | tf_op jit(solution)/shard_map/all_to_all | solution.py:607
  218.6 1.4 step.1
  (140 shorter events, 29.5 us)
Async XLA Ops:
  9.6 40.7 %copy-start.2 = (bf16[256,1024]{1,0:T(8,128)(2,1)S(1)}, bf16[256,1024]{1,0:T(8,128)(2,1)}, u32[]{:S(2)}) copy-start(bf16[256,1024]{1,0:T(8,128)(2,1)} %get-tuple-element.56.k_ref) | copy-start | bytes 1572868
  9.7 40.7 %copy-start.3 = (bf16[256,1024]{1,0:T(8,128)(2,1)S(1)}, bf16[256,1024]{1,0:T(8,128)(2,1)}, u32[]{:S(2)}) copy-start(bf16[256,1024]{1,0:T(8,128)(2,1)} %get-tuple-element.57.v_ref) | copy-start | bytes 1572868
  9.7 40.7 %copy-start.4 = (bf16[256,1024]{1,0:T(8,128)(2,1)S(1)}, bf16[256,1024]{1,0:T(8,128)(2,1)}, u32[]{:S(2)}) copy-start(bf16[256,1024]{1,0:T(8,128)(2,1)} %get-tuple-element.55.q_ref) | copy-start | bytes 1572868
  9.7 40.7 %copy-start.10 = (f32[256,8]{1,0:T(8,128)S(1)}, f32[256,8]{1,0:T(8,128)}, u32[]{:S(2)}) copy-start(f32[256,8]{1,0:T(8,128)} %get-tuple-element.58.tall_ref) | copy-start | bytes 24580
  9.7 40.7 %copy-start.24 = (f32[8,256]{1,0:T(8,128)S(1)}, f32[8,256]{1,0:T(8,128)}, u32[]{:S(2)}) copy-start(f32[8,256]{1,0:T(8,128)} %get-tuple-element.59.flat_ref) | copy-start | bytes 24580
  9.7 31.8 %all-to-all-start = ((f32[32,40,128]{2,1,0:T(8,128)}), f32[32,40,128]{2,1,0:T(8,128)S(1)}, u32[]{:S(2)}, u32[]{:S(2)}) async-start(f32[32,40,128]{2,1,0:T(8,128)} %get-tuple-element.61), calls=%async_computation | async-start | bytes 1310720 | tf_op jit(solution)/shard_map/all_to_all | solution.py:507
  21.2 14.6 %collective-permute-start = (f32[128,1024]{1,0:T(8,128)}, f32[128,1024]{1,0:T(8,128)S(1)}, u32[]{:S(2)}, u32[]{:S(2)}) collective-permute-start(f32[128,1024]{1,0:T(8,128)} %get-tuple-element.62.refs_0_), channel_id=1, source_target_pairs={{0,64},{32,96},{64,128},{96,160},{128,192},{160,224},{192,0},{224,... | collective-permute-start | bytes 1572872 | tf_op jit(solution)/shard_map/ppermute | solution.py:457
  22.7 13.1 %collective-permute-start.1 = (f32[128,1024]{1,0:T(8,128)}, f32[128,1024]{1,0:T(8,128)S(1)}, u32[]{:S(2)}, u32[]{:S(2)}) collective-permute-start(f32[128,1024]{1,0:T(8,128)} %get-tuple-element.63.refs_1_), channel_id=1, source_target_pairs={{0,192},{32,224},{64,0},{96,32},{128,64},{160,96},{192,128},{224,1... | collective-permute-start | bytes 1572872 | tf_op jit(solution)/shard_map/ppermute | solution.py:457
  42.4 23.1 %all-to-all-start.1 = ((f32[32,32,128]{2,1,0:T(8,128)}), f32[32,32,128]{2,1,0:T(8,128)S(1)}, u32[]{:S(2)}, u32[]{:S(2)}) async-start(f32[32,32,128]{2,1,0:T(8,128)} %get-tuple-element.64), calls=%async_computation.1 | async-start | bytes 1048576 | tf_op jit(solution)/shard_map/all_to_all | solution.py:511
  48.1 12.5 %collective-permute-start.3 = (f32[128,1024]{1,0:T(8,128)}, f32[128,1024]{1,0:T(8,128)}, u32[]{:S(2)}, u32[]{:S(2)}) collective-permute-start(f32[128,1024]{1,0:T(8,128)} %get-tuple-element.62.refs_0_), channel_id=1, source_target_pairs={{0,192},{32,224},{64,0},{96,32},{128,64},{160,96},{192,128},{224,1... | collective-permute-start | bytes 1572872 | tf_op jit(solution)/shard_map/ppermute | solution.py:457
  50.4 13.6 %collective-permute-start.2 = (f32[128,1024]{1,0:T(8,128)}, f32[128,1024]{1,0:T(8,128)S(1)}, u32[]{:S(2)}, u32[]{:S(2)}) collective-permute-start(f32[128,1024]{1,0:T(8,128)} %get-tuple-element.63.refs_1_), channel_id=1, source_target_pairs={{0,64},{32,96},{64,128},{96,160},{128,192},{160,224},{192,0},{224,... | collective-permute-start | bytes 1572872 | tf_op jit(solution)/shard_map/ppermute | solution.py:457
  50.4 34.1 %copy-start.22 = (s32[2]{0:T(128)S(1)}, s32[2]{0:T(128)}, u32[]{:S(2)}) copy-start(s32[2]{0:T(128)} %pad_add_fusion.at_ref) | copy-start | bytes 28
  50.4 34.1 %copy-start.23 = (f32[1,8,256]{2,1,0:T(8,128)S(1)}, f32[1,8,256]{2,1,0:T(8,128)}, u32[]{:S(2)}) copy-start(f32[1,8,256]{2,1,0:T(8,128)} %param.5) | copy-start | bytes 24580
  71.4 21.1 %copy-start.8 = (bf16[256,1024]{1,0:T(8,128)(2,1)}, bf16[256,1024]{1,0:T(8,128)(2,1)S(1)}, u32[]{:S(2)}) copy-start(bf16[256,1024]{1,0:T(8,128)(2,1)S(1)} %get-tuple-element.66.dout_ref) | copy-start | bytes 1572868
  71.4 25.0 %all-to-all-start.2 = ((f32[32,32,128]{2,1,0:T(8,128)}), f32[32,32,128]{2,1,0:T(8,128)S(1)}, u32[]{:S(2)}, u32[]{:S(2)}) async-start(f32[32,32,128]{2,1,0:T(8,128)} %copy-done.18), calls=%async_computation.2 | async-start | bytes 1048576 | tf_op jit(solution)/shard_map/all_to_all | solution.py:524
  81.2 12.2 %collective-permute-start.4 = (f32[128,1024]{1,0:T(8,128)}, f32[128,1024]{1,0:T(8,128)S(1)}, u32[]{:S(2)}, u32[]{:S(2)}) collective-permute-start(f32[128,1024]{1,0:T(8,128)} %copy-done.28), channel_id=1, source_target_pairs={{0,64},{32,96},{64,128},{96,160},{128,192},{160,224},{192,0},{224,... | collective-permute-start | bytes 1572872 | tf_op jit(solution)/shard_map/ppermute | solution.py:457
  81.3 12.1 %collective-permute-start.5 = (f32[128,1024]{1,0:T(8,128)}, f32[128,1024]{1,0:T(8,128)S(1)}, u32[]{:S(2)}, u32[]{:S(2)}) collective-permute-start(f32[128,1024]{1,0:T(8,128)} %copy-done.27), channel_id=1, source_target_pairs={{0,192},{32,224},{64,0},{96,32},{128,64},{160,96},{192,128},{224,1... | collective-permute-start | bytes 1572872 | tf_op jit(solution)/shard_map/ppermute | solution.py:457
  87.0 20.0 %collective-permute-start.14 = (f32[4,392,128]{2,1,0:T(8,128)}, f32[4,392,128]{2,1,0:T(8,128)}, u32[]{:S(2)}, u32[]{:S(2)}) collective-permute-start(f32[4,392,128]{2,1,0:T(8,128)} %get-tuple-element.82), channel_id=1, source_target_pairs={{0,32},{32,0},{64,96},{96,64},{128,160},{160,128},{192,224},{224,1... | collective-permute-start | bytes 2408456 | tf_op jit(solution)/shard_map/ppermute | solution.py:457
  87.0 19.0 %collective-permute-start.6 = (f32[128,1024]{1,0:T(8,128)}, f32[128,1024]{1,0:T(8,128)}, u32[]{:S(2)}, u32[]{:S(2)}) collective-permute-start(f32[128,1024]{1,0:T(8,128)} %get-tuple-element.62.refs_0_), channel_id=1, source_target_pairs={{0,32},{32,0},{64,96},{96,64},{128,160},{160,128},{192,224},{224,1... | collective-permute-start | bytes 1572872 | tf_op jit(solution)/shard_map/ppermute | solution.py:457
  87.5 19.0 %collective-permute-start.7 = (f32[128,1024]{1,0:T(8,128)}, f32[128,1024]{1,0:T(8,128)}, u32[]{:S(2)}, u32[]{:S(2)}) collective-permute-start(f32[128,1024]{1,0:T(8,128)} %get-tuple-element.63.refs_1_), channel_id=1, source_target_pairs={{0,32},{32,0},{64,96},{96,64},{128,160},{160,128},{192,224},{224,1... | collective-permute-start | bytes 1572872 | tf_op jit(solution)/shard_map/ppermute | solution.py:457
  93.4 13.2 %collective-permute-start.12 = (f32[128,1024]{1,0:T(8,128)}, f32[128,1024]{1,0:T(8,128)}, u32[]{:S(2)}, u32[]{:S(2)}) collective-permute-start(f32[128,1024]{1,0:T(8,128)} %collective-permute-done.3.refs_4_), channel_id=1, source_target_pairs={{0,32},{32,0},{64,96},{96,64},{128,160},{160,128},{192,224},{224,1... | collective-permute-start | bytes 1572872 | tf_op jit(solution)/shard_map/ppermute | solution.py:457
  97.3 26.6 %all-to-all-start.3 = ((f32[32,32,128]{2,1,0:T(8,128)}), f32[32,32,128]{2,1,0:T(8,128)S(1)}, u32[]{:S(2)}, u32[]{:S(2)}) async-start(f32[32,32,128]{2,1,0:T(8,128)} %copy-done.17), calls=%async_computation.3 | async-start | bytes 1048576 | tf_op jit(solution)/shard_map/all_to_all | solution.py:548
  105.7 5.5 %collective-permute-start.8 = (f32[128,1024]{1,0:T(8,128)}, f32[128,1024]{1,0:T(8,128)S(1)}, u32[]{:S(2)}, u32[]{:S(2)}) collective-permute-start(f32[128,1024]{1,0:T(8,128)} %copy-done.28), channel_id=1, source_target_pairs={{0,32},{32,0},{64,96},{96,64},{128,160},{160,128},{192,224},{224,1... | collective-permute-start | bytes 1572872 | tf_op jit(solution)/shard_map/ppermute | solution.py:457
  106.0 5.2 %collective-permute-start.9 = (f32[128,1024]{1,0:T(8,128)}, f32[128,1024]{1,0:T(8,128)S(1)}, u32[]{:S(2)}, u32[]{:S(2)}) collective-permute-start(f32[128,1024]{1,0:T(8,128)} %copy-done.29), channel_id=1, source_target_pairs={{0,32},{32,0},{64,96},{96,64},{128,160},{160,128},{192,224},{224,1... | collective-permute-start | bytes 1572872 | tf_op jit(solution)/shard_map/ppermute | solution.py:457
  106.5 9.0 %collective-permute-start.13 = (f32[128,1024]{1,0:T(8,128)}, f32[128,1024]{1,0:T(8,128)S(1)}, u32[]{:S(2)}, u32[]{:S(2)}) collective-permute-start(f32[128,1024]{1,0:T(8,128)} %copy-done.27), channel_id=1, source_target_pairs={{0,32},{32,0},{64,96},{96,64},{128,160},{160,128},{192,224},{224,1... | collective-permute-start | bytes 1572872 | tf_op jit(solution)/shard_map/ppermute | solution.py:457
  106.6 8.9 %collective-permute-start.10 = (f32[128,1024]{1,0:T(8,128)}, f32[128,1024]{1,0:T(8,128)S(1)}, u32[]{:S(2)}, u32[]{:S(2)}) collective-permute-start(f32[128,1024]{1,0:T(8,128)} %copy-done.30), channel_id=1, source_target_pairs={{0,32},{32,0},{64,96},{96,64},{128,160},{160,128},{192,224},{224,1... | collective-permute-start | bytes 1572872 | tf_op jit(solution)/shard_map/ppermute | solution.py:457
  107.0 8.5 %collective-permute-start.11 = (f32[128,1024]{1,0:T(8,128)}, f32[128,1024]{1,0:T(8,128)S(1)}, u32[]{:S(2)}, u32[]{:S(2)}) collective-permute-start(f32[128,1024]{1,0:T(8,128)} %copy-done.31), channel_id=1, source_target_pairs={{0,32},{32,0},{64,96},{96,64},{128,160},{160,128},{192,224},{224,1... | collective-permute-start | bytes 1572872 | tf_op jit(solution)/shard_map/ppermute | solution.py:457
  111.2 16.8 %collective-permute-start.15 = (f32[2,392,128]{2,1,0:T(8,128)}, f32[2,392,128]{2,1,0:T(8,128)}, u32[]{:S(2)}, u32[]{:S(2)}) collective-permute-start(f32[2,392,128]{2,1,0:T(8,128)} %get-tuple-element.84), channel_id=1, source_target_pairs={{0,64},{32,96},{64,128},{96,160},{128,192},{160,224},{192,0},{224,... | collective-permute-start | bytes 1204232 | tf_op jit(solution)/shard_map/ppermute | solution.py:457
  111.2 23.3 %collective-permute-start.16 = (f32[2,392,128]{2,1,0:T(8,128)}, f32[2,392,128]{2,1,0:T(8,128)}, u32[]{:S(2)}, u32[]{:S(2)}) collective-permute-start(f32[2,392,128]{2,1,0:T(8,128)} %get-tuple-element.85), channel_id=1, source_target_pairs={{0,128},{32,160},{64,192},{96,224},{128,0},{160,32},{192,64},{224,... | collective-permute-start | bytes 1204232 | tf_op jit(solution)/shard_map/ppermute | solution.py:457
  115.5 19.0 %collective-permute-start.17 = (f32[2,392,128]{2,1,0:T(8,128)}, f32[2,392,128]{2,1,0:T(8,128)}, u32[]{:S(2)}, u32[]{:S(2)}) collective-permute-start(f32[2,392,128]{2,1,0:T(8,128)} %get-tuple-element.86), channel_id=1, source_target_pairs={{0,192},{32,224},{64,0},{96,32},{128,64},{160,96},{192,128},{224,1... | collective-permute-start | bytes 1204232 | tf_op jit(solution)/shard_map/ppermute | solution.py:457
  125.2 1.6 collective-permute-start.18
  126.8 15.8 %collective-permute-start.19 = (f32[2,128,128]{2,1,0:T(8,128)S(1)}, f32[2,128,128]{2,1,0:T(8,128)S(1)}, u32[]{:S(2)}, u32[]{:S(2)}) collective-permute-start(f32[2,128,128]{2,1,0:T(8,128)S(1)} %get-tuple-element.94), channel_id=1, source_target_pairs={{0,64},{32,96},{64,128},{96,160},{128,192},{160,224},{192,0},{224,... | collective-permute-start | bytes 393224 | tf_op jit(solution)/shard_map/ppermute | solution.py:457
  127.8 14.9 %collective-permute-start.20 = (f32[2,128,128]{2,1,0:T(8,128)S(1)}, f32[2,128,128]{2,1,0:T(8,128)S(1)}, u32[]{:S(2)}, u32[]{:S(2)}) collective-permute-start(f32[2,128,128]{2,1,0:T(8,128)S(1)} %get-tuple-element.95), channel_id=1, source_target_pairs={{0,128},{32,160},{64,192},{96,224},{128,0},{160,32},{192,64},{224,... | collective-permute-start | bytes 393224 | tf_op jit(solution)/shard_map/ppermute | solution.py:457
  128.0 14.6 %collective-permute-start.21 = (f32[2,128,128]{2,1,0:T(8,128)S(1)}, f32[2,128,128]{2,1,0:T(8,128)S(1)}, u32[]{:S(2)}, u32[]{:S(2)}) collective-permute-start(f32[2,128,128]{2,1,0:T(8,128)S(1)} %get-tuple-element.96), channel_id=1, source_target_pairs={{0,192},{32,224},{64,0},{96,32},{128,64},{160,96},{192,128},{224,1... | collective-permute-start | bytes 393224 | tf_op jit(solution)/shard_map/ppermute | solution.py:457
  148.4 15.6 %collective-permute-start.22 = (f32[384,256]{1,0:T(8,128)S(1)}, f32[384,256]{1,0:T(8,128)S(1)}, u32[]{:S(2)}, u32[]{:S(2)}) collective-permute-start(f32[384,256]{1,0:T(8,128)S(1)} %term.4), channel_id=1, source_target_pairs={{0,16},{1,17},{2,18},{3,19},{4,20},{5,21},{6,22},{7,23},{8,24},{9,... | collective-permute-start | bytes 1179656 | tf_op jit(solution)/shard_map/ppermute | solution.py:451
  151.5 17.1 %collective-permute-start.23 = (f32[384,256]{1,0:T(8,128)S(1)}, f32[384,256]{1,0:T(8,128)S(1)}, u32[]{:S(2)}, u32[]{:S(2)}) collective-permute-start(f32[384,256]{1,0:T(8,128)S(1)} %term.5), channel_id=1, source_target_pairs={{0,8},{1,9},{2,10},{3,11},{4,12},{5,13},{6,14},{7,15},{8,16},{9,17... | collective-permute-start | bytes 1179656 | tf_op jit(solution)/shard_map/ppermute | solution.py:451
  152.1 16.6 %collective-permute-start.24 = (f32[384,256]{1,0:T(8,128)S(1)}, f32[384,256]{1,0:T(8,128)S(1)}, u32[]{:S(2)}, u32[]{:S(2)}) collective-permute-start(f32[384,256]{1,0:T(8,128)S(1)} %term.6), channel_id=1, source_target_pairs={{0,24},{1,25},{2,26},{3,27},{4,28},{5,29},{6,30},{7,31},{8,0},{9,1... | collective-permute-start | bytes 1179656 | tf_op jit(solution)/shard_map/ppermute | solution.py:451
  169.5 10.7 %collective-permute-start.25 = (f32[32,384]{1,0:T(8,128)S(1)}, f32[32,384]{1,0:T(8,128)S(1)}, u32[]{:S(2)}, u32[]{:S(2)}) collective-permute-start(f32[32,384]{1,0:T(8,128)S(1)} %get-tuple-element.100), channel_id=1, source_target_pairs={{0,1},{1,2},{2,3},{3,4},{4,5},{5,6},{6,7},{7,0},{8,9},{9,10},{10,1... | collective-permute-start | bytes 147464 | tf_op jit(solution)/shard_map/ppermute | solution.py:448
  171.0 11.6 %collective-permute-start.26 = (f32[32,384]{1,0:T(8,128)S(1)}, f32[32,384]{1,0:T(8,128)S(1)}, u32[]{:S(2)}, u32[]{:S(2)}) collective-permute-start(f32[32,384]{1,0:T(8,128)S(1)} %get-tuple-element.101), channel_id=1, source_target_pairs={{0,2},{1,3},{2,4},{3,5},{4,6},{5,7},{6,0},{7,1},{8,10},{9,11},{10,... | collective-permute-start | bytes 147464 | tf_op jit(solution)/shard_map/ppermute | solution.py:448
  174.6 10.6 %collective-permute-start.27 = (f32[32,384]{1,0:T(8,128)S(1)}, f32[32,384]{1,0:T(8,128)S(1)}, u32[]{:S(2)}, u32[]{:S(2)}) collective-permute-start(f32[32,384]{1,0:T(8,128)S(1)} %get-tuple-element.102), channel_id=1, source_target_pairs={{0,3},{1,4},{2,5},{3,6},{4,7},{5,0},{6,1},{7,2},{8,11},{9,12},{10,... | collective-permute-start | bytes 147464 | tf_op jit(solution)/shard_map/ppermute | solution.py:448
  175.2 10.1 %collective-permute-start.28 = (f32[32,384]{1,0:T(8,128)S(1)}, f32[32,384]{1,0:T(8,128)S(1)}, u32[]{:S(2)}, u32[]{:S(2)}) collective-permute-start(f32[32,384]{1,0:T(8,128)S(1)} %get-tuple-element.103), channel_id=1, source_target_pairs={{0,4},{1,5},{2,6},{3,7},{4,0},{5,1},{6,2},{7,3},{8,12},{9,13},{10,... | collective-permute-start | bytes 147464 | tf_op jit(solution)/shard_map/ppermute | solution.py:448
  178.5 9.4 %collective-permute-start.29 = (f32[32,384]{1,0:T(8,128)S(1)}, f32[32,384]{1,0:T(8,128)S(1)}, u32[]{:S(2)}, u32[]{:S(2)}) collective-permute-start(f32[32,384]{1,0:T(8,128)S(1)} %get-tuple-element.104), channel_id=1, source_target_pairs={{0,5},{1,6},{2,7},{3,0},{4,1},{5,2},{6,3},{7,4},{8,13},{9,14},{10,... | collective-permute-start | bytes 147464 | tf_op jit(solution)/shard_map/ppermute | solution.py:448
  180.2 7.7 %collective-permute-start.30 = (f32[32,384]{1,0:T(8,128)S(1)}, f32[32,384]{1,0:T(8,128)S(1)}, u32[]{:S(2)}, u32[]{:S(2)}) collective-permute-start(f32[32,384]{1,0:T(8,128)S(1)} %get-tuple-element.105), channel_id=1, source_target_pairs={{0,6},{1,7},{2,0},{3,1},{4,2},{5,3},{6,4},{7,5},{8,14},{9,15},{10,... | collective-permute-start | bytes 147464 | tf_op jit(solution)/shard_map/ppermute | solution.py:448
  182.6 6.6 %collective-permute-start.31 = (f32[32,384]{1,0:T(8,128)S(1)}, f32[32,384]{1,0:T(8,128)S(1)}, u32[]{:S(2)}, u32[]{:S(2)}) collective-permute-start(f32[32,384]{1,0:T(8,128)S(1)} %get-tuple-element.106), channel_id=1, source_target_pairs={{0,7},{1,0},{2,1},{3,2},{4,3},{5,4},{6,5},{7,6},{8,15},{9,8},{10,9... | collective-permute-start | bytes 147464 | tf_op jit(solution)/shard_map/ppermute | solution.py:448
  189.3 1.3 collective-permute-start.32
  190.6 7.8 %collective-permute-start.35 = (f32[2,32,384]{2,1,0:T(8,128)S(1)}, f32[2,32,384]{2,1,0:T(8,128)S(1)}, u32[]{:S(2)}, u32[]{:S(2)}) collective-permute-start(f32[2,32,384]{2,1,0:T(8,128)S(1)} %both.1.refs_0_), channel_id=1, source_target_pairs={{0,192},{32,224},{64,0},{96,32},{128,64},{160,96},{192,128},{224,1... | collective-permute-start | bytes 294920 | tf_op jit(solution)/shard_map/ppermute | solution.py:457
  193.9 7.1 %collective-permute-start.34 = (f32[2,32,384]{2,1,0:T(8,128)S(1)}, f32[2,32,384]{2,1,0:T(8,128)S(1)}, u32[]{:S(2)}, u32[]{:S(2)}) collective-permute-start(f32[2,32,384]{2,1,0:T(8,128)S(1)} %both.1.refs_0_), channel_id=1, source_target_pairs={{0,128},{32,160},{64,192},{96,224},{128,0},{160,32},{192,64},{224,... | collective-permute-start | bytes 294920 | tf_op jit(solution)/shard_map/ppermute | solution.py:457
  194.0 7.8 %collective-permute-start.33 = (f32[2,32,384]{2,1,0:T(8,128)S(1)}, f32[2,32,384]{2,1,0:T(8,128)S(1)}, u32[]{:S(2)}, u32[]{:S(2)}) collective-permute-start(f32[2,32,384]{2,1,0:T(8,128)S(1)} %both.1.refs_0_), channel_id=1, source_target_pairs={{0,64},{32,96},{64,128},{96,160},{128,192},{160,224},{192,0},{224,... | collective-permute-start | bytes 294920 | tf_op jit(solution)/shard_map/ppermute | solution.py:457
  (31 other events, 116.5 us)

commit v2 on v1

--- a/solution.py
+++ b/solution.py
@@ -120,10 +120,10 @@
     return jnp.sum(jnp.where(lanes == index, table, 0.0), axis=1, keepdims=True)
 
 
-def decay_at(tall, flat_ref, index):
-    length = tall.shape[0]
+def decay_at(column, flat_ref, index):
+    length = column.shape[0]
     causal = ordered(length)
-    spread = column_of(tall, index) - flat_ref[pl.ds(index, 1), :]
+    spread = column - flat_ref[pl.ds(index, 1), :]
     return jnp.where(causal, jnp.exp(jnp.where(causal, spread, 0.0)), 0.0)
 
 
@@ -137,7 +137,7 @@
     def one(head, _):
         at = lanes_at(head, size)
         scores = dot(q_ref[:, at], k_ref[:, at], 1, 1)
-        weights = (scores * decay_at(tall, flat_ref, head)).astype(half)
+        weights = (scores * decay_at(column_of(tall, head), flat_ref, head)).astype(half)
         weights_ref[head] = weights
         intra_ref[:, at] = dot(weights, v_ref[:, at], 1, 0)
 
@@ -243,16 +243,16 @@
     flat_held[...] = flat
     for place, got in enumerate(gots):
         got_held[place] = got[:base, :]
-    entering = jnp.exp(tall)
 
     def one(place, qkv):
         q, k, v = (qkv[:, part * size : (part + 1) * size] for part in range(3))
-        within = decay_at(tall, flat_held, place)
+        column = column_of(tall, place)
+        within = decay_at(column, flat_held, place)
         weights = (dot(q, k, 1, 1) * within).astype(half)
         d_output = got_held[place, :length, :].astype(half)
         state = got_held[place, length:, :].astype(half)
         d_query, dk_ref[place], dv_ref[place] = inner_grads(
-            q, k, v, d_output, weights, state, within, column_of(entering, place)
+            q, k, v, d_output, weights, state, within, jnp.exp(column)
         )
         turned_ref[:, lanes_at(place, length)] = d_query.T
 
@@ -390,13 +390,13 @@
 def inner_kernel(size, q_ref, k_ref, v_ref, dout_ref, weights_ref, state_ref, tall_ref, flat_ref,
                  dq_ref, dk_ref, dv_ref):
     tall = tall_ref[...]
-    entering = jnp.exp(tall)
 
     def one(head, _):
         at = lanes_at(head, size)
+        column = column_of(tall, head)
         dq_ref[:, at], dk_ref[:, at], dv_ref[:, at] = inner_grads(
             q_ref[:, at], k_ref[:, at], v_ref[:, at], dout_ref[:, at], weights_ref[head],
-            state_ref[head].astype(half), decay_at(tall, flat_ref, head), column_of(entering, head)
+            state_ref[head].astype(half), decay_at(column, flat_ref, head), jnp.exp(column)
         )
 
     lax.fori_loop(0, weights_ref.shape[0], one, None)
@@ -457,7 +457,8 @@
         return lax.ppermute(array, "batch", pairs_of)
 
     def line_exchange(arrays):
-        return [arrays[0]] + [along_line(arrays[step], step) for step in range(1, heads)]
+        order = sorted(range(1, heads), key=lambda step: -min(step, heads - step))
+        return [arrays[0]] + [along_line(arrays[step], step) for step in order]
 
     whole = lambda dims: pl.BlockSpec(dims, lambda i: (0,) * len(dims))
     column = pl.BlockSpec((length, wide), lambda i: (0, i))

time: 221 us -> 221 us (level)
  transfers between devices with their start and end apart: 40 -> 40, of which waited for: 17 -> 18; matrix products, arithmetic and copies ran while one was open for 1% -> 1% of each run, Pallas kernels for 15% -> 15%
where the time goes in v2:
time: 221 us; the launch traced here: 220 us
  starting transfers between devices  80.7 us (37%)
  Pallas kernels  53.5 us (24%)
  waiting for transfers between devices  48.2 us (22%)
  blocking collectives  18.8 us (9%)
  local copies, waits for them, and re-layouts  15.2 us (7%)
  other arithmetic  2.62 us (1%)
    pallas_call x22, Pallas kernels, kernel(): pl.pallas_call(body, in_specs=[pl.BlockSpec(memory_space=space(place)) fo...  40.9 us
    ppermute x26, waiting for transfers between devices, along_users(): return lax.ppermute(array, 'batch', pairs_of)  34.7 us
    ppermute x26, starting transfers between devices, along_users(): return lax.ppermute(array, 'batch', pairs_of)  23.2 us
    all_to_all x2, starting transfers between devices, on_device(): got = lax.all_to_all(sums, 'seq', 0, 0)  21.3 us
    all_to_all x1, blocking collectives, on_device(): squares = lax.all_to_all(squares, 'seq', 0, 0)  18.8 us
    ppermute x7, starting transfers between devices, along_line(): return lax.ppermute(array, 'seq', pairs_of)  15.8 us
    unnamed x78, local copies, waits for them, and re-layouts  15.2 us
    all_to_all x1, starting transfers between devices, on_device(): back = lax.all_to_all(entered, 'seq', 0, 0).reshape(heads, size, size)  8.4 us
  transfers between devices with their start and end apart: 40, of which 18 were waited for; matrix products, arithmetic and copies ran while one was open for 1% of the time, Pallas kernels for 15%

profile of v2, /device:TPU:32, one launch (start us, length us, event | category | flops | bytes accessed | tf_op | source)
XLA Modules:
  0.0 220.3 jit_solution(9979504486174300086)
XLA Ops:
  1.3 8.4 %project.1 = (bf16[256,1024]{1,0:T(8,128)(2,1)}, bf16[256,1024]{1,0:T(8,128)(2,1)}, bf16[256,1024]{1,0:T(8,128)(2,1)}, f32[256,8]{1,0:T(8,128)}, f32[8,256]{1,0:...) custom-call(s32[2]{0:T(128)} %pad_add_fusion.at_ref, ...), custom_call_target="tpu_custom_call" | custom-call | flops 1610612736 | bytes 8388608 | tf_op jit(solution)/shard_map/project/pallas_call | solution.py:481
  9.7 11.5 %all-to-all-start = ((f32[32,40,128]{2,1,0:T(8,128)}), f32[32,40,128]{2,1,0:T(8,128)S(1)}, u32[]{:S(2)}, u32[]{:S(2)}) async-start(f32[32,40,128]{2,1,0:T(8,128)} %get-tuple-element.61), calls=%async_computation | async-start | bytes 1310720 | tf_op jit(solution)/shard_map/all_to_all | solution.py:508
  21.2 1.5 collective-permute-start
  22.7 1.8 collective-permute-start.1
  24.5 11.3 %collective-permute-done.refs_2_ = f32[128,1024]{1,0:T(8,128)S(1)} collective-permute-done((f32[128,1024]{1,0:T(8,128)}, f32[128,1024]{1,0:T(8,128)S(1)}, u32[]{:S(2)}, u32[]{:S(2)}) %collective-permute-start) | collective-permute-done | bytes 524320 | tf_op jit(solution)/shard_map/ppermute | solution.py:457
  37.3 4.2 %all-to-all-done.got_ref = f32[32,40,128]{2,1,0:T(8,128)S(1)} async-done(((f32[32,40,128]{2,1,0:T(8,128)}), f32[32,40,128]{2,1,0:T(8,128)S(1)}, u32[]{:S(2)}, u32[]{:S(2)}) %all-to-all-start) | async-done | bytes 655392 | tf_op jit(solution)/shard_map/all_to_all | solution.py:508
  42.4 5.8 %all-to-all-start.1 = ((f32[32,32,128]{2,1,0:T(8,128)}), f32[32,32,128]{2,1,0:T(8,128)S(1)}, u32[]{:S(2)}, u32[]{:S(2)}) async-start(f32[32,32,128]{2,1,0:T(8,128)} %get-tuple-element.64), calls=%async_computation.1 | async-start | bytes 1048576 | tf_op jit(solution)/shard_map/all_to_all | solution.py:512
  48.1 2.2 %collective-permute-start.3 = (f32[128,1024]{1,0:T(8,128)}, f32[128,1024]{1,0:T(8,128)}, u32[]{:S(2)}, u32[]{:S(2)}) collective-permute-start(f32[128,1024]{1,0:T(8,128)} %get-tuple-element.62.refs_0_), channel_id=1, source_target_pairs={{0,192},{32,224},{64,0},{96,32},{128,64},{160,96},{192,128},{224,1... | collective-permute-start | bytes 1572872 | tf_op jit(solution)/shard_map/ppermute | solution.py:457
  50.4 2.7 %weights.1 = (bf16[8,256,256]{2,1,0:T(8,128)(2,1)S(1)}, f32[256,1024]{1,0:T(8,128)S(1)}) custom-call(bf16[256,1024]{1,0:T(8,128)(2,1)S(1)} %copy-done.4, bf16[256,1024]{1,0:T(8,128)(2,1)S(1)} %copy-done.2, bf16[256,1024]{1,0:T(8,128)(2,1)S(1)} %copy-done.3, f32[256,8]{1,0:T(8,128)S(1)} %copy-done.10, f32[8,256]{1,0:T(8,128)S(1)} %copy-done.24), custom_call_target="tpu_custom_call" | custom-call | flops 268435456 | bytes 5242880 | tf_op jit(solution)/shard_map/weights/pallas_call | solution.py:424
  55.1 5.6 %collective-permute-done.3.refs_4_ = f32[128,1024]{1,0:T(8,128)} collective-permute-done((f32[128,1024]{1,0:T(8,128)}, f32[128,1024]{1,0:T(8,128)}, u32[]{:S(2)}, u32[]{:S(2)}) %collective-permute-start.3) | collective-permute-done | bytes 524320 | tf_op jit(solution)/shard_map/ppermute | solution.py:457
  60.7 3.3 %collective-permute-done.2.refs_3_ = f32[128,1024]{1,0:T(8,128)S(1)} collective-permute-done((f32[128,1024]{1,0:T(8,128)}, f32[128,1024]{1,0:T(8,128)S(1)}, u32[]{:S(2)}, u32[]{:S(2)}) %collective-permute-start.2) | collective-permute-done | bytes 524320 | tf_op jit(solution)/shard_map/ppermute | solution.py:457
  65.5 1.2 copy-done.12
  67.8 2.8 %mix.1 = (bf16[256,1024]{1,0:T(8,128)(2,1)}, bf16[256,1024]{1,0:T(8,128)(2,1)S(1)}, f32[32,32,128]{2,1,0:T(8,128)S(1)}) custom-call(bf16[256,1024]{1,0:T(8,128)(2,1)S(1)} %copy-done.4, f32[256,1024]{1,0:T(8,128)S(1)} %copy-done.12, bf16[256,1024]{1,0:T(8,128)(2,1)S(1)} %bitcast.16, f32[256,8]{1,0:T(8,128)S(1)} %copy-done.10, f32[8,128,128]{2,1,0:T(8,128)S(1)} %bitcast.11, ...), custom_call_target="tpu_custom_call" | custom-call | flops 134217728 | bytes 5242880 | tf_op jit(solution)/shard_map/mix/pallas_call | solution.py:424
  71.4 9.8 %all-to-all-start.2 = ((f32[32,32,128]{2,1,0:T(8,128)}), f32[32,32,128]{2,1,0:T(8,128)S(1)}, u32[]{:S(2)}, u32[]{:S(2)}) async-start(f32[32,32,128]{2,1,0:T(8,128)} %copy-done.18), calls=%async_computation.2 | async-start | bytes 1048576 | tf_op jit(solution)/shard_map/all_to_all | solution.py:525
  81.3 3.2 %collective-permute-start.5 = (f32[128,1024]{1,0:T(8,128)}, f32[128,1024]{1,0:T(8,128)S(1)}, u32[]{:S(2)}, u32[]{:S(2)}) collective-permute-start(f32[128,1024]{1,0:T(8,128)} %copy-done.27), channel_id=1, source_target_pairs={{0,192},{32,224},{64,0},{96,32},{128,64},{160,96},{192,128},{224,1... | collective-permute-start | bytes 1572872 | tf_op jit(solution)/shard_map/ppermute | solution.py:457
  84.5 1.6 pack.1
  87.5 4.9 %recall.1 = (bf16[3,256,1024]{2,1,0:T(8,128)(2,1)}, bf16[3,256,384]{2,1,0:T(8,128)(2,1)}, f32[8,128]{1,0:T(8,128)}) custom-call(bf16[1024,384]{1,0:T(8,128)(2,1)} %get-tuple-element.73.weight_ref, f32[8,128]{1,0:T(8,128)} %get-tuple-element.107.after_ref, f32[128,1024]{1,0:T(8,128)} %get-tuple-element.62.refs_0_, f32[128,1024]{1,0:T(8,128)} %get-tuple-element.63.refs_1_, ...), custom_call_target="tpu_custom_call" | custom-call | flops 603979776 | bytes 8388608 | tf_op jit(solution)/shard_map/recall/pallas_call | solution.py:424
  95.0 1.4 all-to-all-done.2.got_ref
  97.3 8.4 %all-to-all-start.3 = ((f32[32,32,128]{2,1,0:T(8,128)}), f32[32,32,128]{2,1,0:T(8,128)S(1)}, u32[]{:S(2)}, u32[]{:S(2)}) async-start(f32[32,32,128]{2,1,0:T(8,128)} %copy-done.17), calls=%async_computation.3 | async-start | bytes 1048576 | tf_op jit(solution)/shard_map/all_to_all | solution.py:549
  107.1 1.1 copy-done.16
  108.3 2.2 pair.2
  111.2 4.2 %collective-permute-start.16 = (f32[2,392,128]{2,1,0:T(8,128)}, f32[2,392,128]{2,1,0:T(8,128)}, u32[]{:S(2)}, u32[]{:S(2)}) collective-permute-start(f32[2,392,128]{2,1,0:T(8,128)} %get-tuple-element.85), channel_id=1, source_target_pairs={{0,128},{32,160},{64,192},{96,224},{128,0},{160,32},{192,64},{224,... | collective-permute-start | bytes 1204232 | tf_op jit(solution)/shard_map/ppermute | solution.py:457
  116.6 6.3 %recall_rest.1 = (bf16[5,256,1024]{2,1,0:T(8,128)(2,1)}, bf16[5,256,384]{2,1,0:T(8,128)(2,1)}, f32[8,128]{1,0:T(8,128)}) custom-call(bf16[1024,384]{1,0:T(8,128)(2,1)} %get-tuple-element.73.weight_ref, f32[8,128]{1,0:T(8,128)} %copy-done.25, f32[128,1024]{1,0:T(8,128)} %copy-done.30, f32[128,1024]{1,0:T(8,128)} %copy-done.31, ...), custom_call_target="tpu_custom_call" | custom-call | flops 1006632960 | bytes 8388608 | tf_op jit(solution)/shard_map/recall_rest/pallas_call | solution.py:424
  125.3 1.5 collective-permute-done.18.came_ref
  128.0 2.5 %collective-permute-start.21 = (f32[2,128,128]{2,1,0:T(8,128)S(1)}, f32[2,128,128]{2,1,0:T(8,128)S(1)}, u32[]{:S(2)}, u32[]{:S(2)}) collective-permute-start(f32[2,128,128]{2,1,0:T(8,128)S(1)} %get-tuple-element.96), channel_id=1, source_target_pairs={{0,192},{32,224},{64,0},{96,32},{128,64},{160,96},{192,128},{224,1... | collective-permute-start | bytes 393224 | tf_op jit(solution)/shard_map/ppermute | solution.py:457
  130.5 3.9 %collective-permute-done.16.refs_2_ = f32[2,392,128]{2,1,0:T(8,128)} collective-permute-done((f32[2,392,128]{2,1,0:T(8,128)}, f32[2,392,128]{2,1,0:T(8,128)}, u32[]{:S(2)}, u32[]{:S(2)}) %collective-permute-start.16) | collective-permute-done | bytes 401440 | tf_op jit(solution)/shard_map/ppermute | solution.py:457
  134.5 1.2 copy-done.5
  136.7 5.9 %owner.1 = (f32[256,8]{1,0:T(8,128)S(1)}, bf16[128,2048]{1,0:T(8,128)(2,1)S(1)}, f32[8,256,128]{2,1,0:T(8,128)S(1)}, f32[8,256,128]{2,1,0:T(8,128)S(1)}) custom-call(bf16[3,256,384]{2,1,0:T(8,128)(2,1)S(1)} %copy-done.6, bf16[5,256,384]{2,1,0:T(8,128)(2,1)S(1)} %copy-done.5, f32[2,392,128]{2,1,0:T(8,128)S(1)} %copy-done.21, ...), custom_call_target="tpu_custom_call" | custom-call | flops 805306368 | bytes 6291456 | tf_op jit(solution)/shard_map/owner/pallas_call | solution.py:424
  142.7 2.2 %late.1.turned_ref = bf16[384,2048]{1,0:T(8,128)(2,1)S(1)} custom-call(bf16[3,256,384]{2,1,0:T(8,128)(2,1)S(1)} %copy-done.6, bf16[5,256,384]{2,1,0:T(8,128)(2,1)S(1)} %copy-done.5, f32[8,256,128]{2,1,0:T(8,128)S(1)} %get-tuple-element.87.dk_ref, f32[8,256,128]{2,1,0:T(8,128)S(1)} %get-tuple-element.88.dv_ref, f32[256,8]{1,0:T(8,128)S(1)} %get-tuple-element.89.tall_ref, ...), custom_call_target="tpu_custom_call" | custom-call | flops 134217728 | bytes 4194304 | tf_op jit(solution)/shard_map/late/pallas_call | solution.py:424
  144.9 1.1 term.6
  146.1 1.2 term.5
  147.3 1.1 term.4
  148.4 3.1 %collective-permute-start.22 = (f32[384,256]{1,0:T(8,128)S(1)}, f32[384,256]{1,0:T(8,128)S(1)}, u32[]{:S(2)}, u32[]{:S(2)}) collective-permute-start(f32[384,256]{1,0:T(8,128)S(1)} %term.4), channel_id=1, source_target_pairs={{0,16},{1,17},{2,18},{3,19},{4,20},{5,21},{6,22},{7,23},{8,24},{9,... | collective-permute-start | bytes 1179656 | tf_op jit(solution)/shard_map/ppermute | solution.py:451
  152.1 2.6 %collective-permute-start.24 = (f32[384,256]{1,0:T(8,128)S(1)}, f32[384,256]{1,0:T(8,128)S(1)}, u32[]{:S(2)}, u32[]{:S(2)}) collective-permute-start(f32[384,256]{1,0:T(8,128)S(1)} %term.6), channel_id=1, source_target_pairs={{0,24},{1,25},{2,26},{3,27},{4,28},{5,29},{6,30},{7,31},{8,0},{9,1... | collective-permute-start | bytes 1179656 | tf_op jit(solution)/shard_map/ppermute | solution.py:451
  154.7 3.8 %inner.1 = (bf16[256,1024]{1,0:T(8,128)(2,1)S(1)}, f32[256,1024]{1,0:T(8,128)S(1)}, f32[256,1024]{1,0:T(8,128)S(1)}) custom-call(bf16[256,1024]{1,0:T(8,128)(2,1)S(1)} %copy-done.4, bf16[256,1024]{1,0:T(8,128)(2,1)S(1)} %copy-done.2, bf16[256,1024]{1,0:T(8,128)(2,1)S(1)} %copy-done.3, bf16[256,1024]{1,0:T(8,128)(2,1)S(1)} %copy-done.9, ...), custom_call_target="tpu_custom_call" | custom-call | flops 671088640 | bytes 6291456 | tf_op jit(solution)/shard_map/inner/pallas_call | solution.py:424
  158.6 4.2 %rows.1.refs_4_ = bf16[256,1024]{1,0:T(8,128)(2,1)} custom-call(bf16[256,1024]{1,0:T(8,128)(2,1)S(1)} %get-tuple-element.68.dq_ref, f32[256,1024]{1,0:T(8,128)S(1)} %get-tuple-element.69.dki_ref, f32[256,1024]{1,0:T(8,128)S(1)} %get-tuple-element.70.dvi_ref, bf16[256,1024]{1,0:T(8,128)(2,1)S(1)} %copy-done.2, bf16[256,1024]{1,0:T(8,128)(2,1)S(1)} %copy-done.3, ...), custom_call_target="tpu_custom_call" | custom-call | flops 1610612736 | bytes 8388608 | tf_op jit(solution)/shard_map/rows/pallas_call | solution.py:574
  164.0 4.7 %collective-permute-done.23.refs_1_ = f32[384,256]{1,0:T(8,128)S(1)} collective-permute-done((f32[384,256]{1,0:T(8,128)S(1)}, f32[384,256]{1,0:T(8,128)S(1)}, u32[]{:S(2)}, u32[]{:S(2)}) %collective-permute-start.23) | collective-permute-done | bytes 393248 | tf_op jit(solution)/shard_map/ppermute | solution.py:451
  169.5 4.6 %collective-permute-start.25 = (f32[32,384]{1,0:T(8,128)S(1)}, f32[32,384]{1,0:T(8,128)S(1)}, u32[]{:S(2)}, u32[]{:S(2)}) collective-permute-start(f32[32,384]{1,0:T(8,128)S(1)} %get-tuple-element.100), channel_id=1, source_target_pairs={{0,4},{1,5},{2,6},{3,7},{4,0},{5,1},{6,2},{7,3},{8,12},{9,13},{10,... | collective-permute-start | bytes 147464 | tf_op jit(solution)/shard_map/ppermute | solution.py:448
  174.6 4.5 %collective-permute-start.27 = (f32[32,384]{1,0:T(8,128)S(1)}, f32[32,384]{1,0:T(8,128)S(1)}, u32[]{:S(2)}, u32[]{:S(2)}) collective-permute-start(f32[32,384]{1,0:T(8,128)S(1)} %get-tuple-element.102), channel_id=1, source_target_pairs={{0,5},{1,6},{2,7},{3,0},{4,1},{5,2},{6,3},{7,4},{8,13},{9,14},{10,... | collective-permute-start | bytes 147464 | tf_op jit(solution)/shard_map/ppermute | solution.py:448
  179.1 4.1 %collective-permute-start.29 = (f32[32,384]{1,0:T(8,128)S(1)}, f32[32,384]{1,0:T(8,128)S(1)}, u32[]{:S(2)}, u32[]{:S(2)}) collective-permute-start(f32[32,384]{1,0:T(8,128)S(1)} %get-tuple-element.104), channel_id=1, source_target_pairs={{0,6},{1,7},{2,0},{3,1},{4,2},{5,3},{6,4},{7,5},{8,14},{9,15},{10,... | collective-permute-start | bytes 147464 | tf_op jit(solution)/shard_map/ppermute | solution.py:448
  183.3 2.0 collective-permute-start.31
  185.4 1.9 collective-permute-done.30.refs_6_
  187.6 1.2 collective-permute-done.32.other_ref
  188.8 3.3 %collective-permute-start.35 = (f32[2,32,384]{2,1,0:T(8,128)S(1)}, f32[2,32,384]{2,1,0:T(8,128)S(1)}, u32[]{:S(2)}, u32[]{:S(2)}) collective-permute-start(f32[2,32,384]{2,1,0:T(8,128)S(1)} %both.1.refs_0_), channel_id=1, source_target_pairs={{0,192},{32,224},{64,0},{96,32},{128,64},{160,96},{192,128},{224,1... | collective-permute-start | bytes 294920 | tf_op jit(solution)/shard_map/ppermute | solution.py:457
  193.1 3.5 %collective-permute-done.35.refs_3_ = f32[2,32,384]{2,1,0:T(8,128)S(1)} collective-permute-done((f32[2,32,384]{2,1,0:T(8,128)S(1)}, f32[2,32,384]{2,1,0:T(8,128)S(1)}, u32[]{:S(2)}, u32[]{:S(2)}) %collective-permute-start.35) | collective-permute-done | bytes 98336 | tf_op jit(solution)/shard_map/ppermute | solution.py:457
  196.6 2.7 %collective-permute-done.34.refs_2_ = f32[2,32,384]{2,1,0:T(8,128)S(1)} collective-permute-done((f32[2,32,384]{2,1,0:T(8,128)S(1)}, f32[2,32,384]{2,1,0:T(8,128)S(1)}, u32[]{:S(2)}, u32[]{:S(2)}) %collective-permute-start.34) | collective-permute-done | bytes 98336 | tf_op jit(solution)/shard_map/ppermute | solution.py:457
  200.0 18.8 %all_to_all.25.squares_ref = f32[32,8,128]{2,1,0:T(8,128)S(1)} all-to-all(f32[32,8,128]{2,1,0:T(8,128)S(1)} %square.1), channel_id=1, replica_groups=mesh['batch'=8,'seq'=32] {'seq'}, dimensions={0} | all-to-all | bytes 262144 | tf_op jit(solution)/shard_map/all_to_all | solution.py:608
  218.9 1.4 step.1
  (140 shorter events, 26.3 us)
Async XLA Ops:
  9.6 40.7 %copy-start.2 = (bf16[256,1024]{1,0:T(8,128)(2,1)S(1)}, bf16[256,1024]{1,0:T(8,128)(2,1)}, u32[]{:S(2)}) copy-start(bf16[256,1024]{1,0:T(8,128)(2,1)} %get-tuple-element.56.k_ref) | copy-start | bytes 1572868
  9.7 40.7 %copy-start.3 = (bf16[256,1024]{1,0:T(8,128)(2,1)S(1)}, bf16[256,1024]{1,0:T(8,128)(2,1)}, u32[]{:S(2)}) copy-start(bf16[256,1024]{1,0:T(8,128)(2,1)} %get-tuple-element.57.v_ref) | copy-start | bytes 1572868
  9.7 40.7 %copy-start.4 = (bf16[256,1024]{1,0:T(8,128)(2,1)S(1)}, bf16[256,1024]{1,0:T(8,128)(2,1)}, u32[]{:S(2)}) copy-start(bf16[256,1024]{1,0:T(8,128)(2,1)} %get-tuple-element.55.q_ref) | copy-start | bytes 1572868
  9.7 40.7 %copy-start.10 = (f32[256,8]{1,0:T(8,128)S(1)}, f32[256,8]{1,0:T(8,128)}, u32[]{:S(2)}) copy-start(f32[256,8]{1,0:T(8,128)} %get-tuple-element.58.tall_ref) | copy-start | bytes 24580
  9.7 40.7 %copy-start.24 = (f32[8,256]{1,0:T(8,128)S(1)}, f32[8,256]{1,0:T(8,128)}, u32[]{:S(2)}) copy-start(f32[8,256]{1,0:T(8,128)} %get-tuple-element.59.flat_ref) | copy-start | bytes 24580
  9.7 31.8 %all-to-all-start = ((f32[32,40,128]{2,1,0:T(8,128)}), f32[32,40,128]{2,1,0:T(8,128)S(1)}, u32[]{:S(2)}, u32[]{:S(2)}) async-start(f32[32,40,128]{2,1,0:T(8,128)} %get-tuple-element.61), calls=%async_computation | async-start | bytes 1310720 | tf_op jit(solution)/shard_map/all_to_all | solution.py:508
  21.2 14.6 %collective-permute-start = (f32[128,1024]{1,0:T(8,128)}, f32[128,1024]{1,0:T(8,128)S(1)}, u32[]{:S(2)}, u32[]{:S(2)}) collective-permute-start(f32[128,1024]{1,0:T(8,128)} %get-tuple-element.62.refs_0_), channel_id=1, source_target_pairs={{0,64},{32,96},{64,128},{96,160},{128,192},{160,224},{192,0},{224,... | collective-permute-start | bytes 1572872 | tf_op jit(solution)/shard_map/ppermute | solution.py:457
  22.7 13.1 %collective-permute-start.1 = (f32[128,1024]{1,0:T(8,128)}, f32[128,1024]{1,0:T(8,128)S(1)}, u32[]{:S(2)}, u32[]{:S(2)}) collective-permute-start(f32[128,1024]{1,0:T(8,128)} %get-tuple-element.63.refs_1_), channel_id=1, source_target_pairs={{0,192},{32,224},{64,0},{96,32},{128,64},{160,96},{192,128},{224,1... | collective-permute-start | bytes 1572872 | tf_op jit(solution)/shard_map/ppermute | solution.py:457
  42.4 23.1 %all-to-all-start.1 = ((f32[32,32,128]{2,1,0:T(8,128)}), f32[32,32,128]{2,1,0:T(8,128)S(1)}, u32[]{:S(2)}, u32[]{:S(2)}) async-start(f32[32,32,128]{2,1,0:T(8,128)} %get-tuple-element.64), calls=%async_computation.1 | async-start | bytes 1048576 | tf_op jit(solution)/shard_map/all_to_all | solution.py:512
  48.1 12.5 %collective-permute-start.3 = (f32[128,1024]{1,0:T(8,128)}, f32[128,1024]{1,0:T(8,128)}, u32[]{:S(2)}, u32[]{:S(2)}) collective-permute-start(f32[128,1024]{1,0:T(8,128)} %get-tuple-element.62.refs_0_), channel_id=1, source_target_pairs={{0,192},{32,224},{64,0},{96,32},{128,64},{160,96},{192,128},{224,1... | collective-permute-start | bytes 1572872 | tf_op jit(solution)/shard_map/ppermute | solution.py:457
  50.4 13.6 %collective-permute-start.2 = (f32[128,1024]{1,0:T(8,128)}, f32[128,1024]{1,0:T(8,128)S(1)}, u32[]{:S(2)}, u32[]{:S(2)}) collective-permute-start(f32[128,1024]{1,0:T(8,128)} %get-tuple-element.63.refs_1_), channel_id=1, source_target_pairs={{0,64},{32,96},{64,128},{96,160},{128,192},{160,224},{192,0},{224,... | collective-permute-start | bytes 1572872 | tf_op jit(solution)/shard_map/ppermute | solution.py:457
  50.4 34.1 %copy-start.22 = (s32[2]{0:T(128)S(1)}, s32[2]{0:T(128)}, u32[]{:S(2)}) copy-start(s32[2]{0:T(128)} %pad_add_fusion.at_ref) | copy-start | bytes 28
  50.4 34.1 %copy-start.23 = (f32[1,8,256]{2,1,0:T(8,128)S(1)}, f32[1,8,256]{2,1,0:T(8,128)}, u32[]{:S(2)}) copy-start(f32[1,8,256]{2,1,0:T(8,128)} %param.5) | copy-start | bytes 24580
  71.4 21.1 %copy-start.8 = (bf16[256,1024]{1,0:T(8,128)(2,1)}, bf16[256,1024]{1,0:T(8,128)(2,1)S(1)}, u32[]{:S(2)}) copy-start(bf16[256,1024]{1,0:T(8,128)(2,1)S(1)} %get-tuple-element.66.dout_ref) | copy-start | bytes 1572868
  71.4 25.0 %all-to-all-start.2 = ((f32[32,32,128]{2,1,0:T(8,128)}), f32[32,32,128]{2,1,0:T(8,128)S(1)}, u32[]{:S(2)}, u32[]{:S(2)}) async-start(f32[32,32,128]{2,1,0:T(8,128)} %copy-done.18), calls=%async_computation.2 | async-start | bytes 1048576 | tf_op jit(solution)/shard_map/all_to_all | solution.py:525
  81.2 12.2 %collective-permute-start.4 = (f32[128,1024]{1,0:T(8,128)}, f32[128,1024]{1,0:T(8,128)S(1)}, u32[]{:S(2)}, u32[]{:S(2)}) collective-permute-start(f32[128,1024]{1,0:T(8,128)} %copy-done.28), channel_id=1, source_target_pairs={{0,64},{32,96},{64,128},{96,160},{128,192},{160,224},{192,0},{224,... | collective-permute-start | bytes 1572872 | tf_op jit(solution)/shard_map/ppermute | solution.py:457
  81.3 12.1 %collective-permute-start.5 = (f32[128,1024]{1,0:T(8,128)}, f32[128,1024]{1,0:T(8,128)S(1)}, u32[]{:S(2)}, u32[]{:S(2)}) collective-permute-start(f32[128,1024]{1,0:T(8,128)} %copy-done.27), channel_id=1, source_target_pairs={{0,192},{32,224},{64,0},{96,32},{128,64},{160,96},{192,128},{224,1... | collective-permute-start | bytes 1572872 | tf_op jit(solution)/shard_map/ppermute | solution.py:457
  87.0 20.0 %collective-permute-start.14 = (f32[4,392,128]{2,1,0:T(8,128)}, f32[4,392,128]{2,1,0:T(8,128)}, u32[]{:S(2)}, u32[]{:S(2)}) collective-permute-start(f32[4,392,128]{2,1,0:T(8,128)} %get-tuple-element.82), channel_id=1, source_target_pairs={{0,32},{32,0},{64,96},{96,64},{128,160},{160,128},{192,224},{224,1... | collective-permute-start | bytes 2408456 | tf_op jit(solution)/shard_map/ppermute | solution.py:457
  87.0 19.0 %collective-permute-start.6 = (f32[128,1024]{1,0:T(8,128)}, f32[128,1024]{1,0:T(8,128)}, u32[]{:S(2)}, u32[]{:S(2)}) collective-permute-start(f32[128,1024]{1,0:T(8,128)} %get-tuple-element.62.refs_0_), channel_id=1, source_target_pairs={{0,32},{32,0},{64,96},{96,64},{128,160},{160,128},{192,224},{224,1... | collective-permute-start | bytes 1572872 | tf_op jit(solution)/shard_map/ppermute | solution.py:457
  87.5 19.0 %collective-permute-start.7 = (f32[128,1024]{1,0:T(8,128)}, f32[128,1024]{1,0:T(8,128)}, u32[]{:S(2)}, u32[]{:S(2)}) collective-permute-start(f32[128,1024]{1,0:T(8,128)} %get-tuple-element.63.refs_1_), channel_id=1, source_target_pairs={{0,32},{32,0},{64,96},{96,64},{128,160},{160,128},{192,224},{224,1... | collective-permute-start | bytes 1572872 | tf_op jit(solution)/shard_map/ppermute | solution.py:457
  93.4 13.2 %collective-permute-start.12 = (f32[128,1024]{1,0:T(8,128)}, f32[128,1024]{1,0:T(8,128)}, u32[]{:S(2)}, u32[]{:S(2)}) collective-permute-start(f32[128,1024]{1,0:T(8,128)} %collective-permute-done.3.refs_4_), channel_id=1, source_target_pairs={{0,32},{32,0},{64,96},{96,64},{128,160},{160,128},{192,224},{224,1... | collective-permute-start | bytes 1572872 | tf_op jit(solution)/shard_map/ppermute | solution.py:457
  97.3 26.6 %all-to-all-start.3 = ((f32[32,32,128]{2,1,0:T(8,128)}), f32[32,32,128]{2,1,0:T(8,128)S(1)}, u32[]{:S(2)}, u32[]{:S(2)}) async-start(f32[32,32,128]{2,1,0:T(8,128)} %copy-done.17), calls=%async_computation.3 | async-start | bytes 1048576 | tf_op jit(solution)/shard_map/all_to_all | solution.py:549
  105.7 5.5 %collective-permute-start.8 = (f32[128,1024]{1,0:T(8,128)}, f32[128,1024]{1,0:T(8,128)S(1)}, u32[]{:S(2)}, u32[]{:S(2)}) collective-permute-start(f32[128,1024]{1,0:T(8,128)} %copy-done.28), channel_id=1, source_target_pairs={{0,32},{32,0},{64,96},{96,64},{128,160},{160,128},{192,224},{224,1... | collective-permute-start | bytes 1572872 | tf_op jit(solution)/shard_map/ppermute | solution.py:457
  106.0 5.2 %collective-permute-start.9 = (f32[128,1024]{1,0:T(8,128)}, f32[128,1024]{1,0:T(8,128)S(1)}, u32[]{:S(2)}, u32[]{:S(2)}) collective-permute-start(f32[128,1024]{1,0:T(8,128)} %copy-done.29), channel_id=1, source_target_pairs={{0,32},{32,0},{64,96},{96,64},{128,160},{160,128},{192,224},{224,1... | collective-permute-start | bytes 1572872 | tf_op jit(solution)/shard_map/ppermute | solution.py:457
  106.5 9.0 %collective-permute-start.13 = (f32[128,1024]{1,0:T(8,128)}, f32[128,1024]{1,0:T(8,128)S(1)}, u32[]{:S(2)}, u32[]{:S(2)}) collective-permute-start(f32[128,1024]{1,0:T(8,128)} %copy-done.27), channel_id=1, source_target_pairs={{0,32},{32,0},{64,96},{96,64},{128,160},{160,128},{192,224},{224,1... | collective-permute-start | bytes 1572872 | tf_op jit(solution)/shard_map/ppermute | solution.py:457
  106.6 8.9 %collective-permute-start.10 = (f32[128,1024]{1,0:T(8,128)}, f32[128,1024]{1,0:T(8,128)S(1)}, u32[]{:S(2)}, u32[]{:S(2)}) collective-permute-start(f32[128,1024]{1,0:T(8,128)} %copy-done.30), channel_id=1, source_target_pairs={{0,32},{32,0},{64,96},{96,64},{128,160},{160,128},{192,224},{224,1... | collective-permute-start | bytes 1572872 | tf_op jit(solution)/shard_map/ppermute | solution.py:457
  107.0 8.5 %collective-permute-start.11 = (f32[128,1024]{1,0:T(8,128)}, f32[128,1024]{1,0:T(8,128)S(1)}, u32[]{:S(2)}, u32[]{:S(2)}) collective-permute-start(f32[128,1024]{1,0:T(8,128)} %copy-done.31), channel_id=1, source_target_pairs={{0,32},{32,0},{64,96},{96,64},{128,160},{160,128},{192,224},{224,1... | collective-permute-start | bytes 1572872 | tf_op jit(solution)/shard_map/ppermute | solution.py:457
  111.2 16.8 %collective-permute-start.15 = (f32[2,392,128]{2,1,0:T(8,128)}, f32[2,392,128]{2,1,0:T(8,128)}, u32[]{:S(2)}, u32[]{:S(2)}) collective-permute-start(f32[2,392,128]{2,1,0:T(8,128)} %get-tuple-element.84), channel_id=1, source_target_pairs={{0,64},{32,96},{64,128},{96,160},{128,192},{160,224},{192,0},{224,... | collective-permute-start | bytes 1204232 | tf_op jit(solution)/shard_map/ppermute | solution.py:457
  111.2 23.3 %collective-permute-start.16 = (f32[2,392,128]{2,1,0:T(8,128)}, f32[2,392,128]{2,1,0:T(8,128)}, u32[]{:S(2)}, u32[]{:S(2)}) collective-permute-start(f32[2,392,128]{2,1,0:T(8,128)} %get-tuple-element.85), channel_id=1, source_target_pairs={{0,128},{32,160},{64,192},{96,224},{128,0},{160,32},{192,64},{224,... | collective-permute-start | bytes 1204232 | tf_op jit(solution)/shard_map/ppermute | solution.py:457
  115.5 19.0 %collective-permute-start.17 = (f32[2,392,128]{2,1,0:T(8,128)}, f32[2,392,128]{2,1,0:T(8,128)}, u32[]{:S(2)}, u32[]{:S(2)}) collective-permute-start(f32[2,392,128]{2,1,0:T(8,128)} %get-tuple-element.86), channel_id=1, source_target_pairs={{0,192},{32,224},{64,0},{96,32},{128,64},{160,96},{192,128},{224,1... | collective-permute-start | bytes 1204232 | tf_op jit(solution)/shard_map/ppermute | solution.py:457
  125.2 1.6 collective-permute-start.18
  126.8 15.8 %collective-permute-start.19 = (f32[2,128,128]{2,1,0:T(8,128)S(1)}, f32[2,128,128]{2,1,0:T(8,128)S(1)}, u32[]{:S(2)}, u32[]{:S(2)}) collective-permute-start(f32[2,128,128]{2,1,0:T(8,128)S(1)} %get-tuple-element.94), channel_id=1, source_target_pairs={{0,64},{32,96},{64,128},{96,160},{128,192},{160,224},{192,0},{224,... | collective-permute-start | bytes 393224 | tf_op jit(solution)/shard_map/ppermute | solution.py:457
  127.8 14.9 %collective-permute-start.20 = (f32[2,128,128]{2,1,0:T(8,128)S(1)}, f32[2,128,128]{2,1,0:T(8,128)S(1)}, u32[]{:S(2)}, u32[]{:S(2)}) collective-permute-start(f32[2,128,128]{2,1,0:T(8,128)S(1)} %get-tuple-element.95), channel_id=1, source_target_pairs={{0,128},{32,160},{64,192},{96,224},{128,0},{160,32},{192,64},{224,... | collective-permute-start | bytes 393224 | tf_op jit(solution)/shard_map/ppermute | solution.py:457
  128.0 14.6 %collective-permute-start.21 = (f32[2,128,128]{2,1,0:T(8,128)S(1)}, f32[2,128,128]{2,1,0:T(8,128)S(1)}, u32[]{:S(2)}, u32[]{:S(2)}) collective-permute-start(f32[2,128,128]{2,1,0:T(8,128)S(1)} %get-tuple-element.96), channel_id=1, source_target_pairs={{0,192},{32,224},{64,0},{96,32},{128,64},{160,96},{192,128},{224,1... | collective-permute-start | bytes 393224 | tf_op jit(solution)/shard_map/ppermute | solution.py:457
  148.4 15.5 %collective-permute-start.22 = (f32[384,256]{1,0:T(8,128)S(1)}, f32[384,256]{1,0:T(8,128)S(1)}, u32[]{:S(2)}, u32[]{:S(2)}) collective-permute-start(f32[384,256]{1,0:T(8,128)S(1)} %term.4), channel_id=1, source_target_pairs={{0,16},{1,17},{2,18},{3,19},{4,20},{5,21},{6,22},{7,23},{8,24},{9,... | collective-permute-start | bytes 1179656 | tf_op jit(solution)/shard_map/ppermute | solution.py:451
  151.5 17.1 %collective-permute-start.23 = (f32[384,256]{1,0:T(8,128)S(1)}, f32[384,256]{1,0:T(8,128)S(1)}, u32[]{:S(2)}, u32[]{:S(2)}) collective-permute-start(f32[384,256]{1,0:T(8,128)S(1)} %term.5), channel_id=1, source_target_pairs={{0,8},{1,9},{2,10},{3,11},{4,12},{5,13},{6,14},{7,15},{8,16},{9,17... | collective-permute-start | bytes 1179656 | tf_op jit(solution)/shard_map/ppermute | solution.py:451
  152.1 16.6 %collective-permute-start.24 = (f32[384,256]{1,0:T(8,128)S(1)}, f32[384,256]{1,0:T(8,128)S(1)}, u32[]{:S(2)}, u32[]{:S(2)}) collective-permute-start(f32[384,256]{1,0:T(8,128)S(1)} %term.6), channel_id=1, source_target_pairs={{0,24},{1,25},{2,26},{3,27},{4,28},{5,29},{6,30},{7,31},{8,0},{9,1... | collective-permute-start | bytes 1179656 | tf_op jit(solution)/shard_map/ppermute | solution.py:451
  169.5 13.8 %collective-permute-start.25 = (f32[32,384]{1,0:T(8,128)S(1)}, f32[32,384]{1,0:T(8,128)S(1)}, u32[]{:S(2)}, u32[]{:S(2)}) collective-permute-start(f32[32,384]{1,0:T(8,128)S(1)} %get-tuple-element.100), channel_id=1, source_target_pairs={{0,4},{1,5},{2,6},{3,7},{4,0},{5,1},{6,2},{7,3},{8,12},{9,13},{10,... | collective-permute-start | bytes 147464 | tf_op jit(solution)/shard_map/ppermute | solution.py:448
  174.1 9.2 %collective-permute-start.26 = (f32[32,384]{1,0:T(8,128)S(1)}, f32[32,384]{1,0:T(8,128)S(1)}, u32[]{:S(2)}, u32[]{:S(2)}) collective-permute-start(f32[32,384]{1,0:T(8,128)S(1)} %get-tuple-element.101), channel_id=1, source_target_pairs={{0,3},{1,4},{2,5},{3,6},{4,7},{5,0},{6,1},{7,2},{8,11},{9,12},{10,... | collective-permute-start | bytes 147464 | tf_op jit(solution)/shard_map/ppermute | solution.py:448
  174.6 10.7 %collective-permute-start.27 = (f32[32,384]{1,0:T(8,128)S(1)}, f32[32,384]{1,0:T(8,128)S(1)}, u32[]{:S(2)}, u32[]{:S(2)}) collective-permute-start(f32[32,384]{1,0:T(8,128)S(1)} %get-tuple-element.102), channel_id=1, source_target_pairs={{0,5},{1,6},{2,7},{3,0},{4,1},{5,2},{6,3},{7,4},{8,13},{9,14},{10,... | collective-permute-start | bytes 147464 | tf_op jit(solution)/shard_map/ppermute | solution.py:448
  179.1 6.3 %collective-permute-start.28 = (f32[32,384]{1,0:T(8,128)S(1)}, f32[32,384]{1,0:T(8,128)S(1)}, u32[]{:S(2)}, u32[]{:S(2)}) collective-permute-start(f32[32,384]{1,0:T(8,128)S(1)} %get-tuple-element.103), channel_id=1, source_target_pairs={{0,2},{1,3},{2,4},{3,5},{4,6},{5,7},{6,0},{7,1},{8,10},{9,11},{10,... | collective-permute-start | bytes 147464 | tf_op jit(solution)/shard_map/ppermute | solution.py:448
  179.1 6.3 %collective-permute-start.29 = (f32[32,384]{1,0:T(8,128)S(1)}, f32[32,384]{1,0:T(8,128)S(1)}, u32[]{:S(2)}, u32[]{:S(2)}) collective-permute-start(f32[32,384]{1,0:T(8,128)S(1)} %get-tuple-element.104), channel_id=1, source_target_pairs={{0,6},{1,7},{2,0},{3,1},{4,2},{5,3},{6,4},{7,5},{8,14},{9,15},{10,... | collective-permute-start | bytes 147464 | tf_op jit(solution)/shard_map/ppermute | solution.py:448
  183.3 4.1 %collective-permute-start.30 = (f32[32,384]{1,0:T(8,128)S(1)}, f32[32,384]{1,0:T(8,128)S(1)}, u32[]{:S(2)}, u32[]{:S(2)}) collective-permute-start(f32[32,384]{1,0:T(8,128)S(1)} %get-tuple-element.105), channel_id=1, source_target_pairs={{0,1},{1,2},{2,3},{3,4},{4,5},{5,6},{6,7},{7,0},{8,9},{9,10},{10,1... | collective-permute-start | bytes 147464 | tf_op jit(solution)/shard_map/ppermute | solution.py:448
  183.3 4.2 %collective-permute-start.31 = (f32[32,384]{1,0:T(8,128)S(1)}, f32[32,384]{1,0:T(8,128)S(1)}, u32[]{:S(2)}, u32[]{:S(2)}) collective-permute-start(f32[32,384]{1,0:T(8,128)S(1)} %get-tuple-element.106), channel_id=1, source_target_pairs={{0,7},{1,0},{2,1},{3,2},{4,3},{5,4},{6,5},{7,6},{8,15},{9,8},{10,9... | collective-permute-start | bytes 147464 | tf_op jit(solution)/shard_map/ppermute | solution.py:448
  187.5 1.3 collective-permute-start.32
  188.8 7.8 %collective-permute-start.35 = (f32[2,32,384]{2,1,0:T(8,128)S(1)}, f32[2,32,384]{2,1,0:T(8,128)S(1)}, u32[]{:S(2)}, u32[]{:S(2)}) collective-permute-start(f32[2,32,384]{2,1,0:T(8,128)S(1)} %both.1.refs_0_), channel_id=1, source_target_pairs={{0,192},{32,224},{64,0},{96,32},{128,64},{160,96},{192,128},{224,1... | collective-permute-start | bytes 294920 | tf_op jit(solution)/shard_map/ppermute | solution.py:457
  192.1 7.1 %collective-permute-start.34 = (f32[2,32,384]{2,1,0:T(8,128)S(1)}, f32[2,32,384]{2,1,0:T(8,128)S(1)}, u32[]{:S(2)}, u32[]{:S(2)}) collective-permute-start(f32[2,32,384]{2,1,0:T(8,128)S(1)} %both.1.refs_0_), channel_id=1, source_target_pairs={{0,128},{32,160},{64,192},{96,224},{128,0},{160,32},{192,64},{224,... | collective-permute-start | bytes 294920 | tf_op jit(solution)/shard_map/ppermute | solution.py:457
  192.2 7.8 %collective-permute-start.33 = (f32[2,32,384]{2,1,0:T(8,128)S(1)}, f32[2,32,384]{2,1,0:T(8,128)S(1)}, u32[]{:S(2)}, u32[]{:S(2)}) collective-permute-start(f32[2,32,384]{2,1,0:T(8,128)S(1)} %both.1.refs_0_), channel_id=1, source_target_pairs={{0,64},{32,96},{64,128},{96,160},{128,192},{160,224},{192,0},{224,... | collective-permute-start | bytes 294920 | tf_op jit(solution)/shard_map/ppermute | solution.py:457
  (31 other events, 116.4 us)
